TPU v7x, 512 devices: a whole 4x4x16 slice. The times are simulated.
512 devices in a mesh: panel: 2 (over z_hi), lon: 32 (over y, z_lo), colat: 8 (over x, core).
Axes of the slice: x: 4, y: 4, z: 16 (z_hi: 2, z_lo: 8; z = z_hi * 8 + z_lo), core: 2. Of those that a mesh axis runs over, the one named last changes fastest.
Arguments:
- state_now: float32 [2, 8, 4, 256, 4096], P('panel', None, None, 'colat', 'lon'), may hold values from -1 to 3
- send_row: int32 [2, 32, 8, 128], P('panel', 'lon', 'colat'), may hold values from 0 to 30
- send_col: int32 [2, 32, 8, 128], P('panel', 'lon', 'colat'), may hold values from 0 to 126
- send_weight: float32 [2, 32, 8, 4, 128], P('panel', 'lon', 'colat'), may hold values from 0 to 1, as said below
- ghost_slot: int32 [2, 32, 8, 640], P('panel', 'lon', 'colat'), may hold values from 0 to 32767, as said below
Outputs:
- next_state: float32 [2, 8, 4, 256, 4096], P('panel', None, None, 'colat', 'lon')
Inputs may be any that keep to these rules, and one draw needn't show every extreme that they name: `ghost_slot`: slot (l * 8 + c) * 128 + s belongs to tile (l, c) of the other panel. Every entry of tile (l, c) names a slot of a tile (l2, c2) of the other panel that lies within one index of (l, c) along lon and along colat, counted round (index 0 and the last index are neighbours). Entries of ghost positions that do not lie on the panel's edge are never read. All 128 slots of at least one device are named by edge positions of the other panel; a slot may be named more than once. `send_weight`: the four weights of a slot are non-negative and sum to one.
All inputs are finite; a program needn't handle non-finite values.
Results may differ from a plain program's by a relative error of at most 0.0003.
Values sent between devices are 32-bit elements; how exact they have to be, the bound alone decides.
A program may use at most 128 MiB of HBM per device.

v0:
```python
import math

import jax
import jax.numpy as jnp
from jax import lax
from jax.sharding import PartitionSpec as P

RADIAL_STEP = 0.65 / 511.0
COURANT = 0.3
ROTATION = 300.0
GRAVITY = 300.0
ADIABATIC = 2.0 / 3.0


def with_halo(cells, sides, width):
    for axis, dim in sides:
        count = lax.axis_size(axis)
        ends = count - 1
        head = lax.slice_in_dim(cells, 0, width, axis=dim)
        tail = lax.slice_in_dim(cells, cells.shape[dim] - width, cells.shape[dim], axis=dim)
        cells = jnp.concatenate(
            [
                lax.ppermute(tail, axis, [(i, (i + 1) % count) for i in range(ends)]),
                cells,
                lax.ppermute(head, axis, [((i + 1) % count, i) for i in range(ends)]),
            ],
            axis=dim,
        )
    return cells


def flux_table(values):
    density = values[0]
    moment = values[1:4]
    magnet = values[4:7]
    energy = values[7]
    velocity = moment / density
    magnet_power = jnp.sum(magnet * magnet, axis=0)
    kinetic = 0.5 * jnp.sum(moment * velocity, axis=0)
    pressure = ADIABATIC * (energy - kinetic - 0.5 * magnet_power)
    total_pressure = pressure + 0.5 * magnet_power
    aligned = jnp.sum(velocity * magnet, axis=0)
    identity = jnp.eye(3, dtype=jnp.float32)[:, :, None, None, None]
    momentum_flux = (
        moment[:, None] * velocity[None, :]
        - magnet[:, None] * magnet[None, :]
        + identity * total_pressure
    )
    induction_flux = magnet[:, None] * velocity[None, :] - velocity[:, None] * magnet[None, :]
    energy_flux = (energy + total_pressure) * velocity - magnet * aligned
    return jnp.concatenate([moment[None], momentum_flux, induction_flux, energy_flux[None]], axis=0)


def radial_slope(values):
    interior = (values[..., 2:, :, :] - values[..., :-2, :, :]) / (2.0 * RADIAL_STEP)
    lowest = (values[..., 1:2, :, :] - values[..., 0:1, :, :]) / RADIAL_STEP
    highest = (values[..., -1:, :, :] - values[..., -2:-1, :, :]) / RADIAL_STEP
    return jnp.concatenate([lowest, interior, highest], axis=-3)


def advance_section(padded, row_start, col_start, total_rows, total_cols, panel_index):
    fields, shells, tall, broad = padded.shape
    lat_cells = tall - 4
    lon_cells = broad - 4
    polar_step = 0.5 * math.pi / total_rows
    azimuth_step = 1.5 * math.pi / total_cols
    time_step = COURANT / (
        1.0 / RADIAL_STEP + 1.0 / polar_step + 1.0 / (azimuth_step * math.sin(0.25 * math.pi))
    )
    colatitude = (
        0.25 * math.pi
        + (
            jnp.asarray(row_start).astype(jnp.float32)
            + jnp.arange(lat_cells, dtype=jnp.float32)
            + 0.5
        )
        * polar_step
    )
    longitude = (
        -0.75 * math.pi
        + (
            jnp.asarray(col_start).astype(jnp.float32)
            + jnp.arange(lon_cells, dtype=jnp.float32)
            + 0.5
        )
        * azimuth_step
    )
    radius = 1.0 - (shells - 1 - jnp.arange(shells, dtype=jnp.float32)) * RADIAL_STEP
    polar_sine = jnp.sin(colatitude)[:, None]
    polar_cosine = jnp.cos(colatitude)[:, None]
    azimuth_sine = jnp.sin(longitude)[None, :]
    azimuth_cosine = jnp.cos(longitude)[None, :]
    filled = jnp.ones((lat_cells, lon_cells), jnp.float32)
    radial_unit = jnp.stack(
        [polar_sine * azimuth_cosine, polar_sine * azimuth_sine, polar_cosine * filled]
    )
    polar_unit = jnp.stack(
        [polar_cosine * azimuth_cosine, polar_cosine * azimuth_sine, -polar_sine * filled]
    )
    azimuth_unit = jnp.stack([-azimuth_sine * filled, azimuth_cosine * filled, 0.0 * filled])
    inverse_radius = (1.0 / radius)[:, None, None]
    column_flux = flux_table(padded[:, :, :, 2:-2])
    row_flux = flux_table(padded[:, :, 2:-2, :])
    radial_part = radial_slope(column_flux[:, :, :, 2:-2, :])
    polar_part = (
        column_flux[..., 0:-4, :]
        - 8.0 * column_flux[..., 1:-3, :]
        + 8.0 * column_flux[..., 3:-1, :]
        - column_flux[..., 4:, :]
    ) / (12.0 * polar_step)
    azimuth_part = (
        row_flux[..., 0:-4]
        - 8.0 * row_flux[..., 1:-3]
        + 8.0 * row_flux[..., 3:-1]
        - row_flux[..., 4:]
    ) / (12.0 * azimuth_step)
    divergence = jnp.sum(
        radial_unit[None, :, None] * radial_part
        + polar_unit[None, :, None] * (inverse_radius * polar_part)
        + azimuth_unit[None, :, None] * (inverse_radius / polar_sine * azimuth_part),
        axis=1,
    )
    centre = padded[:, :, 2:-2, 2:-2]
    density = centre[0]
    moment = centre[1:4]
    panel_weight = jnp.asarray(panel_index).astype(jnp.float32)
    spin_second = ROTATION * panel_weight
    spin_third = ROTATION * (1.0 - panel_weight)
    coriolis = 2.0 * jnp.stack(
        [
            spin_second * moment[2] - spin_third * moment[1],
            spin_third * moment[0],
            -spin_second * moment[0],
        ]
    )
    moment_rate = -divergence[1:4] - coriolis - GRAVITY * density[None] * radial_unit[:, None]
    energy_rate = -divergence[7] - GRAVITY * jnp.sum(moment * radial_unit[:, None], axis=0)
    rate = jnp.concatenate(
        [-divergence[0:1], moment_rate, -divergence[4:7], energy_rate[None]], axis=0
    )
    return centre + time_step * rate


def mix_slots(flattened, anchor, stride, weight):
    upper_left = jnp.take(flattened, anchor, axis=1)
    upper_right = jnp.take(flattened, anchor + 1, axis=1)
    lower_left = jnp.take(flattened, anchor + stride, axis=1)
    lower_right = jnp.take(flattened, anchor + stride + 1, axis=1)
    blended = (
        weight[0] * upper_left
        + weight[1] * upper_right
        + weight[2] * lower_left
        + weight[3] * lower_right
    )
    pieces = blended.reshape(8, blended.shape[0] // 8, blended.shape[1])
    rotated = jnp.stack(
        [pieces[0], -pieces[1], pieces[3], pieces[2], -pieces[4], pieces[6], pieces[5], pieces[7]]
    )
    return rotated.reshape(blended.shape)


def pick_slots(shard_block, wanted):
    breadth = shard_block.shape[1]
    inside = (wanted >= 0) & (wanted < breadth)
    picked = jnp.take(shard_block, jnp.clip(wanted, 0, breadth - 1), axis=1)
    return jnp.where(inside[None, :], picked, 0.0)


def body(state_now, send_row, send_col, send_weight, ghost_slot):
    tile_now = state_now[0]
    fields, shells, lat_cells, lon_cells = tile_now.shape
    lon_count = lax.axis_size("lon")
    colat_count = lax.axis_size("colat")
    colat_at = lax.axis_index("colat")
    lon_at = lax.axis_index("lon")
    capacity = send_row.shape[-1]
    anchor = send_row[0, 0, 0] * lon_cells + send_col[0, 0, 0]
    slot_values = mix_slots(
        tile_now.reshape(fields * shells, lat_cells * lon_cells),
        anchor,
        lon_cells,
        send_weight[0, 0, 0],
    )
    padded = with_halo(tile_now, (("lon", 3), ("colat", 2)), 2)
    wanted = ghost_slot[0, 0, 0]
    other_panel = 1 - lax.axis_index("panel")
    target = wanted + other_panel * (lon_count * colat_count * capacity)
    ghosts = pick_slots(
        lax.all_gather(slot_values, ("panel", "lon", "colat"), axis=1, tiled=True), target
    )
    ghosts = ghosts.reshape(fields, shells, -1)
    north_strip = ghosts[:, :, 0 : 2 * lon_cells].reshape(fields, shells, 2, lon_cells)
    south_strip = ghosts[:, :, 2 * lon_cells : 4 * lon_cells].reshape(fields, shells, 2, lon_cells)
    west_strip = ghosts[:, :, 4 * lon_cells : 4 * lon_cells + 2 * lat_cells].reshape(
        fields, shells, lat_cells, 2
    )
    east_strip = ghosts[:, :, 4 * lon_cells + 2 * lat_cells :].reshape(fields, shells, lat_cells, 2)
    padded = padded.at[:, :, 0:2, 2 : lon_cells + 2].set(
        jnp.where(colat_at == 0, north_strip, padded[:, :, 0:2, 2 : lon_cells + 2])
    )
    padded = padded.at[:, :, lat_cells + 2 : lat_cells + 4, 2 : lon_cells + 2].set(
        jnp.where(
            colat_at == colat_count - 1,
            south_strip,
            padded[:, :, lat_cells + 2 : lat_cells + 4, 2 : lon_cells + 2],
        )
    )
    padded = padded.at[:, :, 2 : lat_cells + 2, 0:2].set(
        jnp.where(lon_at == 0, west_strip, padded[:, :, 2 : lat_cells + 2, 0:2])
    )
    padded = padded.at[:, :, 2 : lat_cells + 2, lon_cells + 2 : lon_cells + 4].set(
        jnp.where(
            lon_at == lon_count - 1,
            east_strip,
            padded[:, :, 2 : lat_cells + 2, lon_cells + 2 : lon_cells + 4],
        )
    )
    result = advance_section(
        padded,
        colat_at * lat_cells,
        lon_at * lon_cells,
        lat_cells * colat_count,
        lon_cells * lon_count,
        lax.axis_index("panel"),
    )
    return result[None]


def solution(mesh):
    placed = (
        P("panel", None, None, "colat", "lon"),
        P("panel", "lon", "colat", None),
        P("panel", "lon", "colat", None),
        P("panel", "lon", "colat", None, None),
        P("panel", "lon", "colat", None),
    )
    return jax.shard_map(
        body,
        mesh=mesh,
        in_specs=placed,
        out_specs=P("panel", None, None, "colat", "lon"),
        check_vma=False,
    )
```

profile of v0, /device:TPU:1, one launch (start us, length us, event | category | flops | bytes accessed | tf_op | source)
XLA Modules:
  0.0 940.9 jit_solution(16580893597833844261)
XLA Ops:
  6.5 0.7 compare_and_fusion.4
  7.2 1.4 copy.195
  8.6 0.6 copy.159
  9.2 0.6 gather_fusion.3
  9.9 0.6 gather_fusion.4
  10.5 0.6 gather_fusion.1
  11.2 0.6 gather_fusion.2
  12.9 0.7 copy.164
  13.9 4.4 collective-permute-start
  18.3 1.3 collective-permute-start.1
  19.9 0.6 fusion.58
  20.6 0.8 and_reduce_fusion.1
  21.8 4.1 collective-permute-done
  25.9 16.2 %collective-permute-done.1 = f32[8,4,32,2]{3,2,1,0:T(8,128)S(1)} collective-permute-done((f32[8,4,32,2]{3,2,1,0:T(8,128)S(1)}, f32[8,4,32,2]{3,2,1,0:T(8,128)S(1)}, u32[]{:S(2)}, u32[]{:S(2)}) %collective-permute-start.1) | collective-permute-done | bytes 8224 | tf_op jit(solution)/shard_map/ppermute | solution.py:25
  42.1 0.3 pad_maximum_fusion.5
  42.4 6.8 collective-permute-start.2
  49.3 2.4 collective-permute-start.3
  51.7 3.3 collective-permute-done.3
  55.1 0.6 pad_maximum_fusion.2
  55.7 818.5 %all-gather.2.cloned.1.call-done = f32[32,65536]{0,1:T(8,128)} async-done(((f32[32,128]{0,1:T(8,128)}), f32[32,65536]{0,1:T(8,128)}) %all-gather.2.cloned.1.call-update) | async-done | bytes 8388624 | tf_op jit(solution)/shard_map/all_gather | solution.py:189
  874.2 12.2 %gather_fusion = f32[640,32]{1,0:T(8,128)S(1)} fusion(f32[32,65536]{0,1:T(8,128)} %all-gather.2.cloned.1.call-done, s32[1024]{0:T(1024)S(1)} %pad_clamp_fusion), kind=kCustom, calls=%fused_computation.4 | custom fusion | bytes 166400 | tf_op jit(solution)/shard_map/jit(_take)/gather | solution.py:165
  886.7 2.1 fusion.46
  888.8 11.2 %scatter.14 = f32[8,4,36,132]{3,2,1,0:T(8,128)S(1)} dynamic-update-slice(f32[8,4,36,132]{3,2,1,0:T(8,128)S(1)} %pad_maximum_fusion.2, f32[8,4,2,128]{3,2,1,0:T(2,128)S(1)} %fusion.46, s32[]{:T(128)} %constant.192.clone.1, s32[]{:T(128)} %constant.192.clone.1, s32[]{:T(128)} %bitcast.21, s32[]{:T(128)} %bitcast.22) | dynamic-update-slice | bytes 65540 | tf_op jit(solution)/shard_map/scatter | solution.py:198
  900.1 0.9 copy.168
  901.1 9.8 %scatter.15 = f32[8,4,36,132]{3,2,1,0:T(8,128)S(1)} dynamic-update-slice(f32[8,4,36,132]{3,2,1,0:T(8,128)S(1)} %scatter.14, f32[8,4,2,128]{3,2,1,0:T(2,128)S(1)} %slice_select_fusion.2, s32[]{:T(128)} %constant.192.clone.1, s32[]{:T(128)} %constant.192.clone.1, s32[]{:T(128)} %constant.209.clone.1, s32[]{:T(128)} %constant.194.clone.1) | dynamic-update-slice | bytes 65540 | tf_op jit(solution)/shard_map/scatter | solution.py:201
  911.0 3.6 scatter.16
  914.7 0.9 copy.170
  915.8 12.6 %scatter.19 = f32[8,4,36,132]{3,2,1,0:T(8,128)S(1)} dynamic-update-slice(f32[8,4,36,132]{3,2,1,0:T(8,128)S(1)} %scatter.16, f32[8,4,32,2]{3,2,1,0:T(8,128)S(1)} %slice_select_fusion, s32[]{:T(128)} %constant.192.clone.1, s32[]{:T(128)} %constant.192.clone.1, s32[]{:T(128)} %constant.194.clone.1, s32[]{:T(128)} %constant.213.clone.1) | dynamic-update-slice | bytes 16388 | tf_op jit(solution)/shard_map/scatter | solution.py:211
  930.5 0.4 multiply_add_fusion
  930.9 0.4 pad_maximum_fusion
  931.3 1.6 fusion.3
  933.0 1.0 fusion.12
  (83 shorter events, 5.1 us)
Async XLA Ops:
  6.5 867.6 %all-gather.2.cloned.1.call-start = ((), (), s32[]{:S(2)}) async-start(), calls=%async_computation | async-start | bytes 33619968 | tf_op jit(solution)/shard_map/all_gather | solution.py:189
  8.6 3.2 copy-start.2
  9.2 4.4 copy-start
  12.5 7.4 copy-start.1
  12.5 8.1 copy-start.3
  13.9 12.1 %collective-permute-start = (f32[8,4,32,2]{3,2,1,0:T(8,128)S(1)}, f32[8,4,32,2]{3,2,1,0:T(8,128)S(1)}, u32[]{:S(2)}, u32[]{:S(2)}) collective-permute-start(f32[8,4,32,2]{3,2,1,0:T(8,128)S(1)} %get-tuple-element.90), channel_id=1, source_target_pairs={{0,8},{8,16},{16,24},{24,32},{32,40},{40,48},{48,56},{56,64},{64,7... | collective-permute-start | bytes 24584 | tf_op jit(solution)/shard_map/ppermute | solution.py:23
  18.3 23.9 %collective-permute-start.1 = (f32[8,4,32,2]{3,2,1,0:T(8,128)S(1)}, f32[8,4,32,2]{3,2,1,0:T(8,128)S(1)}, u32[]{:S(2)}, u32[]{:S(2)}) collective-permute-start(f32[8,4,32,2]{3,2,1,0:T(8,128)S(1)} %get-tuple-element.91), channel_id=1, source_target_pairs={{8,0},{16,8},{24,16},{32,24},{40,32},{48,40},{56,48},{64,56},{72,6... | collective-permute-start | bytes 24584 | tf_op jit(solution)/shard_map/ppermute | solution.py:25
  42.4 9.3 collective-permute-start.2
  49.3 5.8 collective-permute-start.3
Sparse Core Ops, SparseCore 0:
  13.8 860.3 all-gather.1
where the time goes:
time: 946 us; the launch traced here: 941 us
  waiting for transfers between devices  842 us (89%)
  local copies, waits for them, and re-layouts  58.8 us (6%)
  starting transfers between devices  14.9 us (2%)
  between operations  13.9 us (1%)
  other arithmetic  11.2 us (1%)
    all_gather x1, waiting for transfers between devices, body(): lax.all_gather(slot_values, ('panel', 'lon', 'colat'), axis=1, tiled=True)  818 us
    ppermute x2, waiting for transfers between devices, with_halo(): lax.ppermute(head, axis, [((i + 1) % count, i) for i in range(ends)])  19.5 us
  transfers between devices with their start and end apart: 5, of which 4 were waited for; matrix products, arithmetic and copies ran while one was open for 0% of the time, Pallas kernels for 0%

commit v1 on v0

v1 whole, which is shorter than its diff:
```python
import math

import jax
import jax.numpy as jnp
from jax import lax
from jax.experimental import pallas as pl
from jax.experimental.pallas import tpu as pltpu
from jax.sharding import PartitionSpec as P

RADIAL_STEP = 0.65 / 511.0
COURANT = 0.3
ROTATION = 300.0
GRAVITY = 300.0
ADIABATIC = 2.0 / 3.0

FIELDS = 8
SHELLS = 4
CT = 32
CP = 128
SLOTS = 128
TALL = SHELLS * CT
MESH = pl.DeviceIdType.MESH
AROUND = [(dl, dc) for dl in (-1, 0, 1) for dc in (-1, 0, 1)]
TURNED = [(0, 1.0), (1, -1.0), (3, 1.0), (2, 1.0), (4, -1.0), (6, 1.0), (5, 1.0), (7, 1.0)]


def lanes_at(values, index):
    return jnp.take_along_axis(values, index, axis=1, mode="promise_in_bounds")


def cell_terms(u):
    rho, m, b, energy = u[0], u[1:4], u[4:7], u[7]
    inverse = 1.0 / rho
    v = [a * inverse for a in m]
    power = b[0] * b[0] + b[1] * b[1] + b[2] * b[2]
    moving = m[0] * v[0] + m[1] * v[1] + m[2] * v[2]
    pressure = ADIABATIC * (energy - 0.5 * moving - 0.5 * power) + 0.5 * power
    aligned = v[0] * b[0] + v[1] * b[1] + v[2] * b[2]
    return m, b, v, pressure, energy + pressure, aligned, rho


def flux_along(terms, e):
    m, b, v, pressure, enthalpy, aligned, rho = terms
    ve = v[0] * e[0] + v[1] * e[1]
    be = b[0] * e[0] + b[1] * e[1]
    if e[2] is not None:
        ve = ve + v[2] * e[2]
        be = be + b[2] * e[2]
    out = [rho * ve]
    for i in range(3):
        term = m[i] * ve - b[i] * be
        out.append(term if e[i] is None else term + pressure * e[i])
    for i in range(3):
        out.append(b[i] * ve - v[i] * be)
    out.append(enthalpy * ve - aligned * be)
    return out


def kernel(
    x_hbm, row_hbm, col_hbm, weight_hbm, ghost_hbm, out_hbm,
    x, rows, cols, weight, wanted,
    slots, slots_in, row_out, row_in, col_out, col_in,
    radial, polar, azimuth, acc,
    in_sem, send_sem, recv_sem, out_sem,
):
    p, l, c = lax.axis_index("panel"), lax.axis_index("lon"), lax.axis_index("colat")
    nl, nc = lax.axis_size("lon"), lax.axis_size("colat")
    ht = 0.5 * math.pi / (nc * CT)
    hp = 1.5 * math.pi / (nl * CP)
    tau = COURANT / (1.0 / RADIAL_STEP + 1.0 / ht + 1.0 / (hp * math.sin(0.25 * math.pi)))

    def wrap(a, n):
        return lax.rem(a + n, n)

    def on_edge(la, ca):
        return (la == 0) | (la == nl - 1) | (ca == 0) | (ca == nc - 1)

    up, down, left, right = c > 0, c < nc - 1, l > 0, l < nl - 1
    edge = on_edge(l, c)
    others = [(wrap(l + dl, nl), wrap(c + dc, nc)) for dl, dc in AROUND]

    loads = [
        pltpu.make_async_copy(src, dst, in_sem.at[i])
        for i, (src, dst) in enumerate(
            ((row_hbm, rows), (col_hbm, cols), (weight_hbm, weight), (ghost_hbm, wanted), (x_hbm, x))
        )
    ]
    for load in loads:
        load.start()

    barrier = pltpu.get_barrier_semaphore()

    def greet(device):
        pl.semaphore_signal(barrier, inc=1, device_id=device, device_id_type=MESH)

    pl.when(up)(lambda: greet((p, l, c - 1)))
    pl.when(down)(lambda: greet((p, l, c + 1)))
    pl.when(left)(lambda: greet((p, l - 1, c)))
    pl.when(right)(lambda: greet((p, l + 1, c)))

    @pl.when(edge)
    def _():
        for la, ca in others:
            greet((1 - p, la, ca))

    for load in loads:
        load.wait()

    row_at = lax.broadcasted_iota(jnp.int32, (CT, CP), 0)
    lane8 = lax.broadcasted_iota(jnp.int32, (8, 128), 1)
    sub8 = lax.broadcasted_iota(jnp.int32, (8, 128), 0)
    lane32 = lax.broadcasted_iota(jnp.int32, (CT, CP), 1)
    first = row_at == rows[0, 0]
    second = row_at == rows[0, 0] + 1
    w = weight[0, 0, 0]
    on_left = jnp.where(first, w[0:1], jnp.where(second, w[2:3], 0.0))
    on_right = jnp.where(first, w[1:2], jnp.where(second, w[3:4], 0.0))
    pick = jnp.broadcast_to(cols[0, 0], (CT, CP))

    def one_shell(k, _):
        at = pl.multiple_of(k * CT, CT)
        for f in range(FIELDS):
            plane = x[f, pl.ds(at, CT), :]
            mixed = on_left * lanes_at(plane, pick) + on_right * lanes_at(plane, pick + 1)
            target, sign = TURNED[f]
            slots[target, pl.ds(k, 1), :] = sign * jnp.sum(mixed, axis=0, keepdims=True)
        return 0

    lax.fori_loop(0, SHELLS, one_shell, 0)

    lanes = lax.broadcasted_iota(jnp.int32, (TALL, CP), 1)
    packed = jnp.zeros((TALL, CP), jnp.float32)
    for f in range(FIELDS):
        for r in range(2):
            row_out[0, f, pl.ds(4 * r, 4), :] = x[f, pl.ds(r, SHELLS, stride=CT), :]
            row_out[1, f, pl.ds(4 * r, 4), :] = x[f, pl.ds(CT - 2 + r, SHELLS, stride=CT), :]
        turned = pltpu.roll(x[f], 2 + 4 * f, 1)
        packed = jnp.where(lanes // 4 == f, turned, packed)
    upright = packed.T
    for f in range(FIELDS):
        col_out[1, f] = upright[4 * f : 4 * f + 2]
        col_out[0, f] = upright[4 * f + 2 : 4 * f + 4]

    def one(flag):
        return flag.astype(jnp.int32)

    expected = one(up) + one(down) + one(left) + one(right)
    for la, ca in others:
        expected = expected + one(on_edge(la, ca))
    pl.semaphore_wait(barrier, expected)

    def remote(src, dst, i, device):
        return pltpu.make_async_remote_copy(
            src_ref=src, dst_ref=dst, send_sem=send_sem.at[i], recv_sem=recv_sem.at[i],
            device_id=device, device_id_type=MESH,
        )

    slot_copies = [
        pltpu.make_async_remote_copy(
            src_ref=slots, dst_ref=slots_in.at[8 - j], send_sem=send_sem.at[j], recv_sem=recv_sem.at[8 - j],
            device_id=(1 - p, la, ca), device_id_type=MESH,
        )
        for j, (la, ca) in enumerate(others)
    ]
    for copy, (la, ca) in zip(slot_copies, others):
        pl.when(on_edge(la, ca))(copy.start)
    to_up = remote(row_out.at[0], row_in.at[1], 9, (p, l, c - 1))
    to_down = remote(row_out.at[1], row_in.at[0], 10, (p, l, c + 1))
    to_left = remote(col_out.at[0], col_in.at[1], 11, (p, l - 1, c))
    to_right = remote(col_out.at[1], col_in.at[0], 12, (p, l + 1, c))
    pl.when(left)(to_left.start)
    pl.when(right)(to_right.start)
    pl.when(up)(to_up.start)
    pl.when(down)(to_down.start)

    row0 = (c * CT).astype(jnp.float32) + 0.5
    col0 = (l * CP).astype(jnp.float32) + 0.5

    def angle_t(row):
        return 0.25 * math.pi + (row + row0) * ht

    def angle_f(col):
        return -0.75 * math.pi + (col + col0) * hp

    theta = angle_t(row_at.astype(jnp.float32))
    phi = angle_f(lane8[0:1].astype(jnp.float32))
    st, ct = jnp.sin(theta), jnp.cos(theta)
    sf = jnp.broadcast_to(jnp.sin(phi), (8, CP))
    cf = jnp.broadcast_to(jnp.cos(phi), (8, CP))
    spin_second = ROTATION * p.astype(jnp.float32)
    spin_third = ROTATION - spin_second

    def one_block(n, _):
        at = pl.multiple_of(n * 8, 8)
        th = angle_t((sub8 + lax.rem(n, CT // 8) * 8).astype(jnp.float32))
        s8, c8 = jnp.sin(th), jnp.cos(th)
        u = [x[f, pl.ds(at, 8), :] for f in range(FIELDS)]
        terms = cell_terms(u)
        er = (s8 * cf, s8 * sf, c8)
        for f, value in enumerate(flux_along(terms, er)):
            radial[f, pl.ds(at, 8), :] = value
        for f, value in enumerate(flux_along(terms, (c8 * cf, c8 * sf, -s8))):
            polar[f, pl.ds(at, 8), :] = value
        for f, value in enumerate(flux_along(terms, (-sf, cf, None))):
            azimuth[f, pl.ds(at, 8), :] = value
        rho, m = u[0], u[1:4]
        turn = (
            spin_second * m[2] - spin_third * m[1], spin_third * m[0], -spin_second * m[0]
        )
        acc[0, pl.ds(at, 8), :] = u[0]
        for i in range(3):
            acc[1 + i, pl.ds(at, 8), :] = m[i] - tau * (2.0 * turn[i] + GRAVITY * (rho * er[i]))
            acc[4 + i, pl.ds(at, 8), :] = u[4 + i]
        acc[7, pl.ds(at, 8), :] = u[7] - (tau * GRAVITY) * (m[0] * er[0] + m[1] * er[1] + m[2] * er[2])
        return 0

    lax.fori_loop(0, TALL // 8, one_block, 0)

    ends = {1: 8.0 / 12.0, 2: -1.0 / 12.0}

    def gives(along, across, n, step):
        even = (ends[n] / step * math.cos(n * step)) * along
        odd = (ends[n] / step * math.sin(n * step)) * across
        return even + odd, odd - even

    radius = [1.0 - (SHELLS - 1 - k) * RADIAL_STEP for k in range(SHELLS)]

    def one_field(f, _):
        fr = [radial[f, pl.ds(CT * k, CT), :] for k in range(SHELLS)]
        for k in range(SHELLS):
            here = pl.ds(CT * k, CT)
            ft, fp = polar[f, here, :], azimuth[f, here, :]
            flat = st * fr[k] + ct * ft
            total_t = jnp.zeros((CT, CP), jnp.float32)
            total_p = total_t
            for n in (1, 2):
                before, after = gives(ft, fr[k], n, ht)
                total_t = total_t + jnp.where(row_at < CT - n, pltpu.roll(before, CT - n, 0), 0.0)
                total_t = total_t + jnp.where(row_at >= n, pltpu.roll(after, n, 0), 0.0)
                before, after = gives(fp, flat, n, hp)
                total_p = total_p + jnp.where(lane32 < CP - n, pltpu.roll(before, CP - n, 1), 0.0)
                total_p = total_p + jnp.where(lane32 >= n, pltpu.roll(after, n, 1), 0.0)
            low, high = max(k - 1, 0), min(k + 1, SHELLS - 1)
            slope = (fr[high] - fr[low]) * (1.0 / ((high - low) * RADIAL_STEP))
            whole = slope + (1.0 / radius[k]) * (total_t + total_p / st)
            acc[f, here, :] = acc[f, here, :] - tau * whole
        return 0

    lax.fori_loop(0, FIELDS, one_field, 0)

    pl.when(left)(to_right.wait_recv)
    pl.when(right)(to_left.wait_recv)
    pl.when(up)(to_down.wait_recv)
    pl.when(down)(to_up.wait_recv)

    def ghosts(put, index):
        owner = index // SLOTS
        lane = lax.rem(index, SLOTS)
        for j, (la, ca) in enumerate(others):
            here = owner == la * nc + ca
            for f in range(FIELDS):
                half = slots_in[j, f]
                put(j, f, here, lanes_at(jnp.concatenate([half, half], axis=0), lane))

    @pl.when(edge)
    def _():
        for j in range(9):
            slot_copies[8 - j].wait_recv()

    def row_ghosts(side):
        def put(j, f, here, value):
            row_in[side, f] = jnp.where(here, value, 0.0 if j == 0 else row_in[side, f])

        two = [wanted[0, 0, :, pl.ds(256 * side + 128 * r, 128)] for r in range(2)]
        ghosts(put, jnp.where(sub8 < 4, two[0], two[1]))

    def col_ghosts(side):
        line = jnp.broadcast_to(wanted[0, 0, :, pl.ds(512, 128)], (8, 128))
        index = lanes_at(line, 64 * side + 2 * lax.rem(lane8, CT) + sub8 // 4)
        found = [None] * FIELDS

        def put(j, f, here, value):
            found[f] = jnp.where(here, value, 0.0 if j == 0 else found[f])

        ghosts(put, index)
        for f in range(FIELDS):
            own = jnp.where(lane8 // CT == lax.rem(sub8, 4), found[f], 0.0)
            col_in[side, f, pl.ds(0, 1), :] = jnp.sum(own[0:4], axis=0, keepdims=True)
            col_in[side, f, pl.ds(1, 1), :] = jnp.sum(own[4:8], axis=0, keepdims=True)

    pl.when(c == 0)(lambda: row_ghosts(0))
    pl.when(c == nc - 1)(lambda: row_ghosts(1))
    pl.when(l == 0)(lambda: col_ghosts(0))
    pl.when(l == nl - 1)(lambda: col_ghosts(1))

    def near(n):
        return tau * ends[n]

    shell8 = lax.rem(sub8, 4).astype(jnp.float32)
    inverse_r = 1.0 / (1.0 - (SHELLS - 1 - shell8) * RADIAL_STEP)
    upper = sub8 < 4
    for side in range(2):
        u = [row_in[side, f] for f in range(FIELDS)]
        terms = cell_terms(u)
        if side == 0:
            jobs = ((0, -near(2), -near(1)), (1, 0.0, -near(2)))
        else:
            jobs = ((CT - 1, near(1), near(2)), (CT - 2, near(2), 0.0))
        for row, one_w, two_w in jobs:
            th = angle_t(jnp.full((8, 128), row, jnp.float32))
            s8, c8 = jnp.sin(th), jnp.cos(th)
            scale = jnp.where(upper, one_w / ht, two_w / ht) * inverse_r
            for f, value in enumerate(flux_along(terms, (c8 * cf, c8 * sf, -s8))):
                value = value * scale
                where = pl.ds(row, SHELLS, stride=CT)
                acc[f, where, :] = acc[f, where, :] - (value[0:4] + value[4:8])

    sub4 = lax.broadcasted_iota(jnp.int32, (4, 128), 0)
    lane4 = lax.broadcasted_iota(jnp.int32, (4, 128), 1)
    u = [jnp.concatenate([col_in[0, f], col_in[1, f]], axis=0) for f in range(FIELDS)]
    terms = cell_terms(u)
    th = angle_t(lax.rem(lane4, CT).astype(jnp.float32))
    shell4 = (lane4 // CT).astype(jnp.float32)
    share = 1.0 / ((1.0 - (SHELLS - 1 - shell4) * RADIAL_STEP) * jnp.sin(th) * hp)
    parts = []
    for from_left, from_right, weights in (
        (0, CP - 1, (-near(2), -near(1), near(1), near(2))),
        (1, CP - 2, (0.0, -near(2), near(2), 0.0)),
    ):
        ph = angle_f(jnp.where(sub4 < 2, from_left, from_right).astype(jnp.float32))
        scale = jnp.where(
            sub4 < 2,
            jnp.where(sub4 == 0, weights[0], weights[1]),
            jnp.where(sub4 == 2, weights[2], weights[3]),
        ) * share
        parts.append([v * scale for v in flux_along(terms, (-jnp.sin(ph), jnp.cos(ph), None))])
    lines = []
    for f in range(FIELDS):
        close, far = parts[0][f], parts[1][f]
        lines += [far[2:3] + far[3:4], close[2:3] + close[3:4], close[0:1] + close[1:2], far[0:1] + far[1:2]]
    stood = jnp.concatenate(lines + [jnp.zeros((TALL - 4 * FIELDS, CP), jnp.float32)], axis=0).T
    rim = (lanes < 2) | (lanes >= CP - 2)
    stores = []
    for f in range(FIELDS):
        shift = (CP - 2 - 4 * f) % CP
        acc[f] = acc[f] - jnp.where(rim, pltpu.roll(stood, shift, 1) if shift else stood, 0.0)
        stores.append(pltpu.make_async_copy(acc.at[f], out_hbm.at[f], out_sem.at[f]))
        stores[-1].start()

    for copy, (la, ca) in zip(slot_copies, others):
        pl.when(on_edge(la, ca))(copy.wait_send)
    pl.when(left)(to_left.wait_send)
    pl.when(right)(to_right.wait_send)
    pl.when(up)(to_up.wait_send)
    pl.when(down)(to_down.wait_send)
    for store in stores:
        store.wait()


def body(state_now, send_row, send_col, send_weight, ghost_slot):
    f32, i32 = jnp.float32, jnp.int32
    out = pl.pallas_call(
        kernel,
        out_shape=jax.ShapeDtypeStruct((FIELDS, TALL, CP), f32),
        in_specs=[pl.BlockSpec(memory_space=pl.ANY)] * 5,
        out_specs=pl.BlockSpec(memory_space=pl.ANY),
        scratch_shapes=[
            pltpu.VMEM((FIELDS, TALL, CP), f32),
            pltpu.VMEM((1, 1, 1, SLOTS), i32),
            pltpu.VMEM((1, 1, 1, SLOTS), i32),
            pltpu.VMEM((1, 1, 1, 4, SLOTS), f32),
            pltpu.VMEM((1, 1, 1, 640), i32),
            pltpu.VMEM((FIELDS, SHELLS, SLOTS), f32),
            pltpu.VMEM((9, FIELDS, SHELLS, SLOTS), f32),
            pltpu.VMEM((2, FIELDS, 8, CP), f32),
            pltpu.VMEM((2, FIELDS, 8, CP), f32),
            pltpu.VMEM((2, FIELDS, 2, TALL), f32),
            pltpu.VMEM((2, FIELDS, 2, TALL), f32),
            pltpu.VMEM((FIELDS, TALL, CP), f32),
            pltpu.VMEM((FIELDS, TALL, CP), f32),
            pltpu.VMEM((FIELDS, TALL, CP), f32),
            pltpu.VMEM((FIELDS, TALL, CP), f32),
            pltpu.SemaphoreType.DMA((5,)),
            pltpu.SemaphoreType.DMA((13,)),
            pltpu.SemaphoreType.DMA((13,)),
            pltpu.SemaphoreType.DMA((FIELDS,)),
        ],
        compiler_params=pltpu.CompilerParams(
            collective_id=0, has_side_effects=True, vmem_limit_bytes=32 * 1024 * 1024
        ),
    )(state_now.reshape(FIELDS, TALL, CP), send_row, send_col, send_weight, ghost_slot)
    return out.reshape(1, FIELDS, SHELLS, CT, CP)


def solution(mesh):
    placed = (
        P("panel", None, None, "colat", "lon"),
        P("panel", "lon", "colat", None),
        P("panel", "lon", "colat", None),
        P("panel", "lon", "colat", None, None),
        P("panel", "lon", "colat", None),
    )
    return jax.shard_map(
        body,
        mesh=mesh,
        in_specs=placed,
        out_specs=P("panel", None, None, "colat", "lon"),
        check_vma=False,
    )
```

time: 946 us -> 32 us (0.03)
  waiting for transfers between devices: 842 us -> 0 us
  local copies, waits for them, and re-layouts: 58.8 us -> 3.87 us
  Pallas kernels: 0 us -> 27.9 us
  starting transfers between devices: 14.9 us -> 0 us
  between operations: 13.9 us -> 0.01 us
  other arithmetic: 11.2 us -> 0 us
    all_gather x1 -> x0, waiting for transfers between devices: 818 us -> none  [body(): lax.all_gather(slot_values, ('panel', 'lon', 'colat'), axis=1, tiled=True)]
    scatter x4 -> x0, local copies, waits for them, and re-layouts: 37.2 us -> none  [the longest x1 12.6 us: body(): padded.at[:, :, 2:lat_cells + 2, lon_cells + 2:lon_cells + 4]]
    pallas_call x0 -> x1, Pallas kernels: none -> 27.9 us  [body(): pl.pallas_call(kernel, out_shape=jax.ShapeDtypeStruct((FIELDS, TALL, CP),...]
    ppermute x4 -> x0, waiting for transfers between devices: 23.6 us -> none  [the longest x2 19.5 us: with_halo(): lax.ppermute(head, axis, [((i + 1) % count, i) for i in range(ends)])]
    gather x7 -> x0, local copies, waits for them, and re-layouts: 14.9 us -> none  [the longest x3 12.4 us: pick_slots(): picked = jnp.take(shard_block, jnp.clip(wanted, 0, breadth - 1), axis=1)]
    ppermute x4 -> x0, starting transfers between devices: 14.9 us -> none  [the longest x2 11.2 us: with_halo(): lax.ppermute(tail, axis, [(i, (i + 1) % count) for i in range(ends)])]
  transfers between devices with their start and end apart: 5 -> 0, of which waited for: 4 -> 0; matrix products, arithmetic and copies ran while one was open for 0% -> 0% of each run, Pallas kernels for 0% -> 0%
where the time goes in v1:
time: 32 us; the launch traced here: 31.8 us
  Pallas kernels  27.9 us (87%)
  local copies, waits for them, and re-layouts  3.87 us (12%)
    pallas_call x1, Pallas kernels, body(): pl.pallas_call(kernel, out_shape=jax.ShapeDtypeStruct((FIELDS, TALL, CP),...  27.9 us
    unnamed x11, local copies, waits for them, and re-layouts  3.87 us

profile of v1, /device:TPU:1, one launch (start us, length us, event | category | flops | bytes accessed | tf_op | source)
XLA Modules:
  0.0 31.8 jit_solution(7369105964253594288)
XLA Ops:
  0.0 0.0 copy-start.4
  0.0 0.0 copy-start.3
  0.0 0.7 %copy-done.4 = s32[1,1,1,128]{3,2,1,0:T(1,128)S(1)} copy-done((s32[1,1,1,128]{3,2,1,0:T(1,128)S(1)}, s32[1,1,1,128]{3,2,1,0:T(1,128)}, u32[]{:S(2)}) %copy-start.4) | copy-done | bytes 536
  0.7 0.0 copy-done.3
  0.7 0.0 copy-start
  0.7 1.0 %copy-done = f32[1,8,4,32,128]{4,3,2,1,0:T(8,128)S(1)} copy-done((f32[1,8,4,32,128]{4,3,2,1,0:T(8,128)S(1)}, f32[1,8,4,32,128]{4,3,2,1,0:T(8,128)}, u32[]{:S(2)}) %copy-start) | copy-done | bytes 524312
  1.7 0.0 copy-start.1
  1.7 0.7 %copy-done.1 = s32[1,1,1,640]{3,2,1,0:T(1,128)S(1)} copy-done((s32[1,1,1,640]{3,2,1,0:T(1,128)S(1)}, s32[1,1,1,640]{3,2,1,0:T(1,128)}, u32[]{:S(2)}) %copy-start.1) | copy-done | bytes 2584
  2.4 0.0 copy-start.2
  2.4 0.7 %copy-done.2 = f32[1,1,1,4,128]{4,3,2,1,0:T(4,128)S(1)} copy-done((f32[1,1,1,4,128]{4,3,2,1,0:T(4,128)S(1)}, f32[1,1,1,4,128]{4,3,2,1,0:T(4,128)}, u32[]{:S(2)}) %copy-start.2) | copy-done | bytes 2072
  3.1 27.9 %shard_map.55 = f32[8,128,128]{2,1,0:T(8,128)S(1)} custom-call(f32[8,128,128]{2,1,0:T(8,128)S(1)} %bitcast.3, s32[1,1,1,128]{3,2,1,0:T(1,128)S(1)} %copy-done.3, s32[1,1,1,128]{3,2,1,0:T(1,128)S(1)} %copy-done.4, f32[1,1,1,4,128]{4,3,2,1,0:T(4,128)S(1)} %copy-done.2, s32[1,1,1,640]{3,2,1,0:T(1,128)S(1)} %copy-done.1), custom_call_target="tpu_custom_call" | custom-call | tf_op jit(solution)/shard_map/pallas_call | solution.py:362
  31.0 0.8 %copy.7 = f32[1,8,4,32,128]{4,3,2,1,0:T(8,128)} copy(f32[1,8,4,32,128]{4,3,2,1,0:T(8,128)S(1)} %bitcast.2) | data formatting | bytes 1048576
Async XLA Ops:
  0.0 0.7 %copy-start.4 = (s32[1,1,1,128]{3,2,1,0:T(1,128)S(1)}, s32[1,1,1,128]{3,2,1,0:T(1,128)}, u32[]{:S(2)}) copy-start(s32[1,1,1,128]{3,2,1,0:T(1,128)} %col_hbm.1) | copy-start | bytes 1540
  0.0 0.7 %copy-start.3 = (s32[1,1,1,128]{3,2,1,0:T(1,128)S(1)}, s32[1,1,1,128]{3,2,1,0:T(1,128)}, u32[]{:S(2)}) copy-start(s32[1,1,1,128]{3,2,1,0:T(1,128)} %row_hbm.1) | copy-start | bytes 1540
  0.7 1.0 %copy-start = (f32[1,8,4,32,128]{4,3,2,1,0:T(8,128)S(1)}, f32[1,8,4,32,128]{4,3,2,1,0:T(8,128)}, u32[]{:S(2)}) copy-start(f32[1,8,4,32,128]{4,3,2,1,0:T(8,128)} %param.5) | copy-start | bytes 1572868
  1.7 0.7 %copy-start.1 = (s32[1,1,1,640]{3,2,1,0:T(1,128)S(1)}, s32[1,1,1,640]{3,2,1,0:T(1,128)}, u32[]{:S(2)}) copy-start(s32[1,1,1,640]{3,2,1,0:T(1,128)} %ghost_hbm.1) | copy-start | bytes 7684
  2.4 0.7 %copy-start.2 = (f32[1,1,1,4,128]{4,3,2,1,0:T(4,128)S(1)}, f32[1,1,1,4,128]{4,3,2,1,0:T(4,128)}, u32[]{:S(2)}) copy-start(f32[1,1,1,4,128]{4,3,2,1,0:T(4,128)} %weight_hbm.1) | copy-start | bytes 6148

commit v2 on v1

--- a/solution.py
+++ b/solution.py
@@ -57,11 +57,11 @@
 
 
 def kernel(
-    x_hbm, row_hbm, col_hbm, weight_hbm, ghost_hbm, out_hbm,
+    x_hbm, row_hbm, col_hbm, weight_hbm, ghost_hbm, acc,
     x, rows, cols, weight, wanted,
     slots, slots_in, row_out, row_in, col_out, col_in,
-    radial, polar, azimuth, acc,
-    in_sem, send_sem, recv_sem, out_sem,
+    radial, polar, azimuth,
+    in_sem, send_sem, recv_sem,
 ):
     p, l, c = lax.axis_index("panel"), lax.axis_index("lon"), lax.axis_index("colat")
     nl, nc = lax.axis_size("lon"), lax.axis_size("colat")
@@ -79,13 +79,14 @@
     edge = on_edge(l, c)
     others = [(wrap(l + dl, nl), wrap(c + dc, nc)) for dl, dc in AROUND]
 
-    loads = [
-        pltpu.make_async_copy(src, dst, in_sem.at[i])
+    small = [
+        pltpu.make_async_copy(src, dst, in_sem.at[FIELDS + i])
         for i, (src, dst) in enumerate(
-            ((row_hbm, rows), (col_hbm, cols), (weight_hbm, weight), (ghost_hbm, wanted), (x_hbm, x))
+            ((row_hbm, rows), (col_hbm, cols), (weight_hbm, weight), (ghost_hbm, wanted))
         )
     ]
-    for load in loads:
+    large = [pltpu.make_async_copy(x_hbm.at[f], x.at[f], in_sem.at[f]) for f in range(FIELDS)]
+    for load in small + large:
         load.start()
 
     barrier = pltpu.get_barrier_semaphore()
@@ -93,17 +94,17 @@
     def greet(device):
         pl.semaphore_signal(barrier, inc=1, device_id=device, device_id_type=MESH)
 
+    @pl.when(edge)
+    def _():
+        for la, ca in others:
+            greet((1 - p, la, ca))
+
+    pl.when(left)(lambda: greet((p, l - 1, c)))
+    pl.when(right)(lambda: greet((p, l + 1, c)))
     pl.when(up)(lambda: greet((p, l, c - 1)))
     pl.when(down)(lambda: greet((p, l, c + 1)))
-    pl.when(left)(lambda: greet((p, l - 1, c)))
-    pl.when(right)(lambda: greet((p, l + 1, c)))
-
-    @pl.when(edge)
-    def _():
-        for la, ca in others:
-            greet((1 - p, la, ca))
-
-    for load in loads:
+
+    for load in small:
         load.wait()
 
     row_at = lax.broadcasted_iota(jnp.int32, (CT, CP), 0)
@@ -116,17 +117,37 @@
     on_left = jnp.where(first, w[0:1], jnp.where(second, w[2:3], 0.0))
     on_right = jnp.where(first, w[1:2], jnp.where(second, w[3:4], 0.0))
     pick = jnp.broadcast_to(cols[0, 0], (CT, CP))
-
-    def one_shell(k, _):
-        at = pl.multiple_of(k * CT, CT)
-        for f in range(FIELDS):
-            plane = x[f, pl.ds(at, CT), :]
+    for f in range(FIELDS):
+        large[f].wait()
+        target, sign = TURNED[f]
+        for k in range(SHELLS):
+            plane = x[f, CT * k : CT * (k + 1), :]
             mixed = on_left * lanes_at(plane, pick) + on_right * lanes_at(plane, pick + 1)
-            target, sign = TURNED[f]
-            slots[target, pl.ds(k, 1), :] = sign * jnp.sum(mixed, axis=0, keepdims=True)
-        return 0
-
-    lax.fori_loop(0, SHELLS, one_shell, 0)
+            slots[target, k : k + 1, :] = sign * jnp.sum(mixed, axis=0, keepdims=True)
+
+    def one(flag):
+        return flag.astype(jnp.int32)
+
+    expected = one(up) + one(down) + one(left) + one(right)
+    for la, ca in others:
+        expected = expected + one(on_edge(la, ca))
+    pl.semaphore_wait(barrier, expected)
+
+    def remote(src, dst, i, device):
+        return pltpu.make_async_remote_copy(
+            src_ref=src, dst_ref=dst, send_sem=send_sem.at[i], recv_sem=recv_sem.at[i],
+            device_id=device, device_id_type=MESH,
+        )
+
+    slot_copies = [
+        pltpu.make_async_remote_copy(
+            src_ref=slots, dst_ref=slots_in.at[8 - j], send_sem=send_sem.at[j], recv_sem=recv_sem.at[8 - j],
+            device_id=(1 - p, la, ca), device_id_type=MESH,
+        )
+        for j, (la, ca) in enumerate(others)
+    ]
+    for copy, (la, ca) in zip(slot_copies, others):
+        pl.when(on_edge(la, ca))(copy.start)
 
     lanes = lax.broadcasted_iota(jnp.int32, (TALL, CP), 1)
     packed = jnp.zeros((TALL, CP), jnp.float32)
@@ -141,29 +162,6 @@
         col_out[1, f] = upright[4 * f : 4 * f + 2]
         col_out[0, f] = upright[4 * f + 2 : 4 * f + 4]
 
-    def one(flag):
-        return flag.astype(jnp.int32)
-
-    expected = one(up) + one(down) + one(left) + one(right)
-    for la, ca in others:
-        expected = expected + one(on_edge(la, ca))
-    pl.semaphore_wait(barrier, expected)
-
-    def remote(src, dst, i, device):
-        return pltpu.make_async_remote_copy(
-            src_ref=src, dst_ref=dst, send_sem=send_sem.at[i], recv_sem=recv_sem.at[i],
-            device_id=device, device_id_type=MESH,
-        )
-
-    slot_copies = [
-        pltpu.make_async_remote_copy(
-            src_ref=slots, dst_ref=slots_in.at[8 - j], send_sem=send_sem.at[j], recv_sem=recv_sem.at[8 - j],
-            device_id=(1 - p, la, ca), device_id_type=MESH,
-        )
-        for j, (la, ca) in enumerate(others)
-    ]
-    for copy, (la, ca) in zip(slot_copies, others):
-        pl.when(on_edge(la, ca))(copy.start)
     to_up = remote(row_out.at[0], row_in.at[1], 9, (p, l, c - 1))
     to_down = remote(row_out.at[1], row_in.at[0], 10, (p, l, c + 1))
     to_left = remote(col_out.at[0], col_in.at[1], 11, (p, l - 1, c))
@@ -248,58 +246,14 @@
 
     lax.fori_loop(0, FIELDS, one_field, 0)
 
-    pl.when(left)(to_right.wait_recv)
-    pl.when(right)(to_left.wait_recv)
-    pl.when(up)(to_down.wait_recv)
-    pl.when(down)(to_up.wait_recv)
-
-    def ghosts(put, index):
-        owner = index // SLOTS
-        lane = lax.rem(index, SLOTS)
-        for j, (la, ca) in enumerate(others):
-            here = owner == la * nc + ca
-            for f in range(FIELDS):
-                half = slots_in[j, f]
-                put(j, f, here, lanes_at(jnp.concatenate([half, half], axis=0), lane))
-
-    @pl.when(edge)
-    def _():
-        for j in range(9):
-            slot_copies[8 - j].wait_recv()
-
-    def row_ghosts(side):
-        def put(j, f, here, value):
-            row_in[side, f] = jnp.where(here, value, 0.0 if j == 0 else row_in[side, f])
-
-        two = [wanted[0, 0, :, pl.ds(256 * side + 128 * r, 128)] for r in range(2)]
-        ghosts(put, jnp.where(sub8 < 4, two[0], two[1]))
-
-    def col_ghosts(side):
-        line = jnp.broadcast_to(wanted[0, 0, :, pl.ds(512, 128)], (8, 128))
-        index = lanes_at(line, 64 * side + 2 * lax.rem(lane8, CT) + sub8 // 4)
-        found = [None] * FIELDS
-
-        def put(j, f, here, value):
-            found[f] = jnp.where(here, value, 0.0 if j == 0 else found[f])
-
-        ghosts(put, index)
-        for f in range(FIELDS):
-            own = jnp.where(lane8 // CT == lax.rem(sub8, 4), found[f], 0.0)
-            col_in[side, f, pl.ds(0, 1), :] = jnp.sum(own[0:4], axis=0, keepdims=True)
-            col_in[side, f, pl.ds(1, 1), :] = jnp.sum(own[4:8], axis=0, keepdims=True)
-
-    pl.when(c == 0)(lambda: row_ghosts(0))
-    pl.when(c == nc - 1)(lambda: row_ghosts(1))
-    pl.when(l == 0)(lambda: col_ghosts(0))
-    pl.when(l == nl - 1)(lambda: col_ghosts(1))
-
     def near(n):
         return tau * ends[n]
 
     shell8 = lax.rem(sub8, 4).astype(jnp.float32)
-    inverse_r = 1.0 / (1.0 - (SHELLS - 1 - shell8) * RADIAL_STEP)
+    inverse_r = 1.0 / ((1.0 - (SHELLS - 1 - shell8) * RADIAL_STEP) * ht)
     upper = sub8 < 4
-    for side in range(2):
+
+    def add_rows(side):
         u = [row_in[side, f] for f in range(FIELDS)]
         terms = cell_terms(u)
         if side == 0:
@@ -309,43 +263,106 @@
         for row, one_w, two_w in jobs:
             th = angle_t(jnp.full((8, 128), row, jnp.float32))
             s8, c8 = jnp.sin(th), jnp.cos(th)
-            scale = jnp.where(upper, one_w / ht, two_w / ht) * inverse_r
+            scale = jnp.where(upper, one_w, two_w) * inverse_r
+            where = pl.ds(row, SHELLS, stride=CT)
             for f, value in enumerate(flux_along(terms, (c8 * cf, c8 * sf, -s8))):
                 value = value * scale
-                where = pl.ds(row, SHELLS, stride=CT)
                 acc[f, where, :] = acc[f, where, :] - (value[0:4] + value[4:8])
 
-    sub4 = lax.broadcasted_iota(jnp.int32, (4, 128), 0)
-    lane4 = lax.broadcasted_iota(jnp.int32, (4, 128), 1)
-    u = [jnp.concatenate([col_in[0, f], col_in[1, f]], axis=0) for f in range(FIELDS)]
-    terms = cell_terms(u)
-    th = angle_t(lax.rem(lane4, CT).astype(jnp.float32))
-    shell4 = (lane4 // CT).astype(jnp.float32)
-    share = 1.0 / ((1.0 - (SHELLS - 1 - shell4) * RADIAL_STEP) * jnp.sin(th) * hp)
-    parts = []
-    for from_left, from_right, weights in (
-        (0, CP - 1, (-near(2), -near(1), near(1), near(2))),
-        (1, CP - 2, (0.0, -near(2), near(2), 0.0)),
-    ):
-        ph = angle_f(jnp.where(sub4 < 2, from_left, from_right).astype(jnp.float32))
-        scale = jnp.where(
-            sub4 < 2,
-            jnp.where(sub4 == 0, weights[0], weights[1]),
-            jnp.where(sub4 == 2, weights[2], weights[3]),
-        ) * share
-        parts.append([v * scale for v in flux_along(terms, (-jnp.sin(ph), jnp.cos(ph), None))])
-    lines = []
-    for f in range(FIELDS):
-        close, far = parts[0][f], parts[1][f]
-        lines += [far[2:3] + far[3:4], close[2:3] + close[3:4], close[0:1] + close[1:2], far[0:1] + far[1:2]]
-    stood = jnp.concatenate(lines + [jnp.zeros((TALL - 4 * FIELDS, CP), jnp.float32)], axis=0).T
     rim = (lanes < 2) | (lanes >= CP - 2)
-    stores = []
-    for f in range(FIELDS):
-        shift = (CP - 2 - 4 * f) % CP
-        acc[f] = acc[f] - jnp.where(rim, pltpu.roll(stood, shift, 1) if shift else stood, 0.0)
-        stores.append(pltpu.make_async_copy(acc.at[f], out_hbm.at[f], out_sem.at[f]))
-        stores[-1].start()
+
+    def add_columns():
+        sub4 = lax.broadcasted_iota(jnp.int32, (4, 128), 0)
+        lane4 = lax.broadcasted_iota(jnp.int32, (4, 128), 1)
+        u = [jnp.concatenate([col_in[0, f], col_in[1, f]], axis=0) for f in range(FIELDS)]
+        terms = cell_terms(u)
+        th = angle_t(lax.rem(lane4, CT).astype(jnp.float32))
+        shell4 = (lane4 // CT).astype(jnp.float32)
+        share = 1.0 / ((1.0 - (SHELLS - 1 - shell4) * RADIAL_STEP) * jnp.sin(th) * hp)
+        parts = []
+        for from_left, from_right, weights in (
+            (0, CP - 1, (-near(2), -near(1), near(1), near(2))),
+            (1, CP - 2, (0.0, -near(2), near(2), 0.0)),
+        ):
+            ph = angle_f(jnp.where(sub4 < 2, from_left, from_right).astype(jnp.float32))
+            scale = jnp.where(
+                sub4 < 2,
+                jnp.where(sub4 == 0, weights[0], weights[1]),
+                jnp.where(sub4 == 2, weights[2], weights[3]),
+            ) * share
+            parts.append([v * scale for v in flux_along(terms, (-jnp.sin(ph), jnp.cos(ph), None))])
+        lines = []
+        for f in range(FIELDS):
+            close, far = parts[0][f], parts[1][f]
+            lines += [far[2:3] + far[3:4], close[2:3] + close[3:4], close[0:1] + close[1:2], far[0:1] + far[1:2]]
+        stood = jnp.concatenate(lines + [jnp.zeros((TALL - 4 * FIELDS, CP), jnp.float32)], axis=0).T
+        for f in range(FIELDS):
+            shift = (CP - 2 - 4 * f) % CP
+            acc[f] = acc[f] - jnp.where(rim, pltpu.roll(stood, shift, 1) if shift else stood, 0.0)
+
+    def ghosts(index, put):
+        owner = index // SLOTS
+        lane = lax.rem(index, SLOTS)
+        here = [owner == la * nc + ca for la, ca in others]
+
+        def one_field(f, _):
+            found = jnp.zeros((8, 128), jnp.float32)
+            for j in range(9):
+                half = slots_in[j, f]
+                found = jnp.where(here[j], lanes_at(jnp.concatenate([half, half], axis=0), lane), found)
+            put(f, found)
+            return 0
+
+        lax.fori_loop(0, FIELDS, one_field, 0)
+
+    def row_ghosts(side):
+        def put(f, found):
+            row_in[side, f] = found
+
+        two = [wanted[0, 0, :, pl.ds(256 * side + 128 * r, 128)] for r in range(2)]
+        ghosts(jnp.where(sub8 < 4, two[0], two[1]), put)
+
+    def column_ghosts(side):
+        def put(f, found):
+            own = jnp.where(lane8 // CT == lax.rem(sub8, 4), found, 0.0)
+            col_in[side, f, pl.ds(0, 1), :] = jnp.sum(own[0:4], axis=0, keepdims=True)
+            col_in[side, f, pl.ds(1, 1), :] = jnp.sum(own[4:8], axis=0, keepdims=True)
+
+        line = jnp.broadcast_to(wanted[0, 0, :, pl.ds(512, 128)], (8, 128))
+        ghosts(lanes_at(line, 64 * side + 2 * lax.rem(lane8, CT) + sub8 // 4), put)
+
+    pl.when(left)(to_right.wait_recv)
+    pl.when(right)(to_left.wait_recv)
+    pl.when(left & right)(add_columns)
+
+    @pl.when(up)
+    def _():
+        to_down.wait_recv()
+        add_rows(0)
+
+    @pl.when(down)
+    def _():
+        to_up.wait_recv()
+        add_rows(1)
+
+    @pl.when(edge)
+    def _():
+        for j in range(9):
+            slot_copies[8 - j].wait_recv()
+
+    pl.when(l == 0)(lambda: column_ghosts(0))
+    pl.when(l == nl - 1)(lambda: column_ghosts(1))
+    pl.when((l == 0) | (l == nl - 1))(add_columns)
+
+    @pl.when(c == 0)
+    def _():
+        row_ghosts(0)
+        add_rows(0)
+
+    @pl.when(c == nc - 1)
+    def _():
+        row_ghosts(1)
+        add_rows(1)
 
     for copy, (la, ca) in zip(slot_copies, others):
         pl.when(on_edge(la, ca))(copy.wait_send)
@@ -353,17 +370,15 @@
     pl.when(right)(to_right.wait_send)
     pl.when(up)(to_up.wait_send)
     pl.when(down)(to_down.wait_send)
-    for store in stores:
-        store.wait()
 
 
 def body(state_now, send_row, send_col, send_weight, ghost_slot):
     f32, i32 = jnp.float32, jnp.int32
     out = pl.pallas_call(
         kernel,
-        out_shape=jax.ShapeDtypeStruct((FIELDS, TALL, CP), f32),
-        in_specs=[pl.BlockSpec(memory_space=pl.ANY)] * 5,
-        out_specs=pl.BlockSpec(memory_space=pl.ANY),
+        out_shape=pltpu.VMEM((FIELDS, TALL, CP), f32),
+        in_specs=[pl.BlockSpec(memory_space=pltpu.HBM)] * 5,
+        out_specs=pl.BlockSpec(memory_space=pltpu.VMEM),
         scratch_shapes=[
             pltpu.VMEM((FIELDS, TALL, CP), f32),
             pltpu.VMEM((1, 1, 1, SLOTS), i32),
@@ -379,16 +394,14 @@
             pltpu.VMEM((FIELDS, TALL, CP), f32),
             pltpu.VMEM((FIELDS, TALL, CP), f32),
             pltpu.VMEM((FIELDS, TALL, CP), f32),
-            pltpu.VMEM((FIELDS, TALL, CP), f32),
-            pltpu.SemaphoreType.DMA((5,)),
+            pltpu.SemaphoreType.DMA((12,)),
             pltpu.SemaphoreType.DMA((13,)),
             pltpu.SemaphoreType.DMA((13,)),
-            pltpu.SemaphoreType.DMA((FIELDS,)),
         ],
         compiler_params=pltpu.CompilerParams(
             collective_id=0, has_side_effects=True, vmem_limit_bytes=32 * 1024 * 1024
         ),
-    )(state_now.reshape(FIELDS, TALL, CP), send_row, send_col, send_weight, ghost_slot)
+    )(*[pltpu.with_memory_space_constraint(a, pltpu.HBM) for a in (state_now.reshape(FIELDS, TALL, CP), send_row, send_col, send_weight, ghost_slot)])
     return out.reshape(1, FIELDS, SHELLS, CT, CP)
 
 

time: 32 us -> 28.3 us (0.88)
  local copies, waits for them, and re-layouts: 3.87 us -> 0.8 us
  Pallas kernels: 27.9 us -> 27.4 us
    unnamed x11 -> x1, local copies, waits for them, and re-layouts: 3.87 us -> 0.8 us
    pallas_call x1, Pallas kernels: 27.9 us -> 27.4 us  [body(): pl.pallas_call(kernel, out_shape=pltpu.VMEM((FIELDS, TALL, CP), f32), in_...]
where the time goes in v2:
time: 28.3 us; the launch traced here: 28.2 us
  Pallas kernels  27.4 us (97%)
  local copies, waits for them, and re-layouts  0.8 us (3%)
    pallas_call x1, Pallas kernels, body(): pl.pallas_call(kernel, out_shape=pltpu.VMEM((FIELDS, TALL, CP), f32), in_...  27.4 us
    unnamed x1, local copies, waits for them, and re-layouts  0.8 us

profile of v2, /device:TPU:1, one launch (start us, length us, event | category | flops | bytes accessed | tf_op | source)
XLA Modules:
  0.0 28.2 jit_solution(10628458929668354364)
XLA Ops:
  0.0 27.4 %shard_map.55 = f32[8,128,128]{2,1,0:T(8,128)S(1)} custom-call(f32[8,128,128]{2,1,0:T(8,128)} %bitcast.3, s32[1,1,1,128]{3,2,1,0:T(1,128)} %row_hbm.1, s32[1,1,1,128]{3,2,1,0:T(1,128)} %col_hbm.1, f32[1,1,1,4,128]{4,3,2,1,0:T(4,128)} %weight_hbm.1, s32[1,1,1,640]{3,2,1,0:T(1,128)} %ghost_hbm.1), custom_call_target="tpu_custom_call" | custom-call | tf_op jit(solution)/shard_map/pallas_call | solution.py:377
  27.4 0.8 %copy.7 = f32[1,8,4,32,128]{4,3,2,1,0:T(8,128)} copy(f32[1,8,4,32,128]{4,3,2,1,0:T(8,128)S(1)} %bitcast.2) | data formatting | bytes 1048576

commit v3 on v2

--- a/solution.py
+++ b/solution.py
@@ -20,6 +20,7 @@
 SLOTS = 128
 TALL = SHELLS * CT
 MESH = pl.DeviceIdType.MESH
+RUN = 8
 AROUND = [(dl, dc) for dl in (-1, 0, 1) for dc in (-1, 0, 1)]
 TURNED = [(0, 1.0), (1, -1.0), (3, 1.0), (2, 1.0), (4, -1.0), (6, 1.0), (5, 1.0), (7, 1.0)]
 
@@ -60,8 +61,8 @@
     x_hbm, row_hbm, col_hbm, weight_hbm, ghost_hbm, acc,
     x, rows, cols, weight, wanted,
     slots, slots_in, row_out, row_in, col_out, col_in,
-    radial, polar, azimuth,
-    in_sem, send_sem, recv_sem,
+    radial, polar, azimuth, picked, named,
+    in_sem, send_sem, recv_sem, told,
 ):
     p, l, c = lax.axis_index("panel"), lax.axis_index("lon"), lax.axis_index("colat")
     nl, nc = lax.axis_size("lon"), lax.axis_size("colat")
@@ -72,12 +73,11 @@
     def wrap(a, n):
         return lax.rem(a + n, n)
 
+    def on_row(ca):
+        return (ca == 0) | (ca == nc - 1)
+
     def on_edge(la, ca):
-        return (la == 0) | (la == nl - 1) | (ca == 0) | (ca == nc - 1)
-
-    up, down, left, right = c > 0, c < nc - 1, l > 0, l < nl - 1
-    edge = on_edge(l, c)
-    others = [(wrap(l + dl, nl), wrap(c + dc, nc)) for dl, dc in AROUND]
+        return (la == 0) | (la == nl - 1) | on_row(ca)
 
     small = [
         pltpu.make_async_copy(src, dst, in_sem.at[FIELDS + i])
@@ -89,20 +89,90 @@
     for load in small + large:
         load.start()
 
+    up, down, left, right = c > 0, c < nc - 1, l > 0, l < nl - 1
+    edge = on_edge(l, c)
+    others = [(wrap(l + dl, nl), wrap(c + dc, nc)) for dl, dc in AROUND]
+
+    late = 4
+    place = lax.rem(l, RUN)
+
+    def passed(panel, tile, la):
+        far = (panel == 1) | ((lax.rem(tile, RUN) >= late) & (lax.rem(la, RUN) != RUN - 1))
+        return far & (tile // RUN == la // RUN)
+
+    flows_out, direct_in, shut_out, shut_in = [], [], [], []
+    to_panel_1 = p == 0
+    for (la, ca), (dl, dc) in zip(others, AROUND):
+        flow, got = on_edge(la, ca), edge
+        if dl:
+            flow = flow & ~(on_row(ca) & passed(1 - p, la, l))
+            got = got & ~(on_row(c) & passed(p, l, la))
+        if dc != 1:
+            flow = flow & ~((p == 1) & (la == 0) & (lax.rem(ca, 2) == 0))
+        if dc != -1:
+            got = got & ~((p == 0) & (l == 0) & (lax.rem(c, 2) == 0))
+        flows_out.append(flow)
+        direct_in.append(got)
+        shut_out.append((p == 1) & (((place == RUN - 1) & (dl <= 0)) | ((place == 0) & (dl == -1))))
+        shut_in.append((p == 0) & (((place == RUN - 1) & (dl >= 0)) | ((place == RUN - 2) & (dl == 1))))
+    row_edge = on_row(c)
+    take_left, take_right = row_edge & left & passed(p, l, l - 1), row_edge & right & passed(p, l, l + 1)
+    pass_left, pass_right = row_edge & left & passed(p, l - 1, l), row_edge & right & passed(p, l + 1, l)
+    mate_gives = (p == 0) & (l == 0) & (lax.rem(c, 2) == 1)
+    mate_takes = (p == 0) & (l == 0) & (lax.rem(c, 2) == 0)
+
+    inner = jnp.clip(c, 2, nc - 3)
+    at_seam = (place == 0) | (place == RUN - 1)
+    at_end = (l == 0) | (l == nl - 1)
+    beside = (c < 2) | (c >= nc - 2)
+    helped_1 = (p == 1) & at_seam & (beside | at_end)
+    helped_0 = (p == 0) & (place == RUN - 1) & (beside | at_end)
+    at_helper = (c == 2) | (c == nc - 3)
+    helper_1 = (p == 1) & at_seam & ~at_end & at_helper
+    helper_0 = (p == 0) & (place == RUN - 1) & ~at_end & at_helper
+    end_helper = (l == nl - 2) & ~beside
+    over_left, over_right = left & (place == 0), right & (place == RUN - 1)
+    seam_by_help = helped_1 & ~at_end
+    near_left, near_right = left & ~(over_left & seam_by_help), right & ~(over_right & seam_by_help)
+
     barrier = pltpu.get_barrier_semaphore()
 
-    def greet(device):
+    def greet(*device):
         pl.semaphore_signal(barrier, inc=1, device_id=device, device_id_type=MESH)
 
-    @pl.when(edge)
-    def _():
-        for la, ca in others:
-            greet((1 - p, la, ca))
-
-    pl.when(left)(lambda: greet((p, l - 1, c)))
-    pl.when(right)(lambda: greet((p, l + 1, c)))
-    pl.when(up)(lambda: greet((p, l, c - 1)))
-    pl.when(down)(lambda: greet((p, l, c + 1)))
+    for j, (la, ca) in enumerate(others):
+        by_help = (p == 1) & (lax.rem(la, RUN) == RUN - 1)
+        to_l = jnp.where(by_help & (la == nl - 1), nl - 2, la)
+        to_c = jnp.where(by_help, jnp.clip(ca, 2, nc - 3), ca)
+        pl.when(direct_in[j] & ~shut_in[j])(lambda: greet(1 - p, to_l, to_c))
+
+    pl.when(near_left)(lambda: greet(p, l - 1, c))
+    pl.when(near_right)(lambda: greet(p, l + 1, c))
+    pl.when(up)(lambda: greet(p, l, c - 1))
+    pl.when(down)(lambda: greet(p, l, c + 1))
+
+    @pl.when(helped_0 | helped_1)
+    def _():
+        greet(p, jnp.where(at_end, nl - 2, l), inner)
+        pl.when(seam_by_help)(lambda: greet(p, jnp.where(place == 0, l - 1, l + 1), inner))
+
+    @pl.when((p == 0) & (l < nl - 1) & row_edge & (place >= RUN - 2))
+    def _():
+        end = l == nl - 2
+        last = jnp.where(end, l, l - place + RUN - 1)
+        for helper in (2, nc - 3):
+            greet(1, last, helper)
+            pl.when(place == RUN - 1)(lambda: greet(1, l + 1, helper))
+
+    @pl.when((p == 0) & (l == nl - 1))
+    def _():
+        for helper in range(2, nc - 2):
+            reach = (c >= helper - 1) & (c <= helper + 1)
+            if helper == 2:
+                reach = (c <= helper + 1) | (c == nc - 1)
+            if helper == nc - 3:
+                reach = (c >= helper - 1) | (c == 0)
+            pl.when(reach)(lambda: greet(1, nl - 2, helper))
 
     for load in small:
         load.wait()
@@ -128,12 +198,16 @@
     def one(flag):
         return flag.astype(jnp.int32)
 
-    expected = one(up) + one(down) + one(left) + one(right)
-    for la, ca in others:
-        expected = expected + one(on_edge(la, ca))
+    expected = one(up) + one(down) + one(near_left) + one(near_right)
+    for flow, shut in zip(flows_out, shut_out):
+        expected = expected + one(flow & ~shut & ~helped_0)
+    expected = expected + one(helper_1) * (6 + 2 * one(place == RUN - 1)) + 8 * one(helper_0)
+    served = jnp.where(at_helper, 3, 1)
+    at_panel_1 = 2 * served + jnp.where(at_helper, 7, 3)
+    expected = expected + one(end_helper) * jnp.where(p == 1, at_panel_1, 7 * served)
     pl.semaphore_wait(barrier, expected)
 
-    def remote(src, dst, i, device):
+    def remote(src, dst, i, *device):
         return pltpu.make_async_remote_copy(
             src_ref=src, dst_ref=dst, send_sem=send_sem.at[i], recv_sem=recv_sem.at[i],
             device_id=device, device_id_type=MESH,
@@ -146,8 +220,35 @@
         )
         for j, (la, ca) in enumerate(others)
     ]
-    for copy, (la, ca) in zip(slot_copies, others):
-        pl.when(on_edge(la, ca))(copy.start)
+
+    def send_slots(wave):
+        for j, (la, ca) in enumerate(others):
+            spot = lax.rem(la, RUN)
+            turn = jnp.where(p == 0, 0, jnp.where(spot == 0, 0, jnp.where(spot < 3, 0, jnp.where(spot < 5, 0, 0))))
+            pl.when(flows_out[j] & ~shut_out[j] & ~helped_0 & (turn == wave))(slot_copies[j].start)
+
+    send_slots(0)
+
+    def tell(*device):
+        pl.semaphore_signal(told, inc=1, device_id=device, device_id_type=MESH)
+
+    @pl.when(helper_0 | helper_1)
+    def _():
+        first = jnp.where(c == 2, 0, nc - 2)
+        tell(p, l, first)
+        tell(p, l, first + 1)
+
+    @pl.when(end_helper)
+    def _():
+        tell(p, nl - 1, c)
+        pl.when(p == 1)(lambda: tell(p, 0, c))
+
+        @pl.when(at_helper)
+        def _():
+            first = jnp.where(c == 2, 0, nc - 2)
+            for more in range(2):
+                tell(p, nl - 1, first + more)
+                pl.when(p == 1)(lambda: tell(p, 0, first + more))
 
     lanes = lax.broadcasted_iota(jnp.int32, (TALL, CP), 1)
     packed = jnp.zeros((TALL, CP), jnp.float32)
@@ -162,12 +263,12 @@
         col_out[1, f] = upright[4 * f : 4 * f + 2]
         col_out[0, f] = upright[4 * f + 2 : 4 * f + 4]
 
-    to_up = remote(row_out.at[0], row_in.at[1], 9, (p, l, c - 1))
-    to_down = remote(row_out.at[1], row_in.at[0], 10, (p, l, c + 1))
-    to_left = remote(col_out.at[0], col_in.at[1], 11, (p, l - 1, c))
-    to_right = remote(col_out.at[1], col_in.at[0], 12, (p, l + 1, c))
-    pl.when(left)(to_left.start)
-    pl.when(right)(to_right.start)
+    to_up = remote(row_out.at[0], row_in.at[1], 9, p, l, c - 1)
+    to_down = remote(row_out.at[1], row_in.at[0], 10, p, l, c + 1)
+    to_left = remote(col_out.at[0], col_in.at[1], 11, p, l - 1, c)
+    to_right = remote(col_out.at[1], col_in.at[0], 12, p, l + 1, c)
+    pl.when(near_left)(to_left.start)
+    pl.when(near_right)(to_right.start)
     pl.when(up)(to_up.start)
     pl.when(down)(to_down.start)
 
@@ -246,6 +347,14 @@
 
     lax.fori_loop(0, FIELDS, one_field, 0)
 
+    @pl.when(helped_0 | helped_1)
+    def _():
+        pl.semaphore_wait(told, 1)
+        pl.when(over_left & seam_by_help)(to_left.start)
+        pl.when(over_right & seam_by_help)(to_right.start)
+        for j in range(9):
+            pl.when(flows_out[j] & (shut_out[j] | helped_0))(slot_copies[j].start)
+
     def near(n):
         return tau * ends[n]
 
@@ -253,8 +362,8 @@
     inverse_r = 1.0 / ((1.0 - (SHELLS - 1 - shell8) * RADIAL_STEP) * ht)
     upper = sub8 < 4
 
-    def add_rows(side):
-        u = [row_in[side, f] for f in range(FIELDS)]
+    def add_rows(side, rim):
+        u = [rim[f] for f in range(FIELDS)]
         terms = cell_terms(u)
         if side == 0:
             jobs = ((0, -near(2), -near(1)), (1, 0.0, -near(2)))
@@ -300,37 +409,6 @@
             shift = (CP - 2 - 4 * f) % CP
             acc[f] = acc[f] - jnp.where(rim, pltpu.roll(stood, shift, 1) if shift else stood, 0.0)
 
-    def ghosts(index, put):
-        owner = index // SLOTS
-        lane = lax.rem(index, SLOTS)
-        here = [owner == la * nc + ca for la, ca in others]
-
-        def one_field(f, _):
-            found = jnp.zeros((8, 128), jnp.float32)
-            for j in range(9):
-                half = slots_in[j, f]
-                found = jnp.where(here[j], lanes_at(jnp.concatenate([half, half], axis=0), lane), found)
-            put(f, found)
-            return 0
-
-        lax.fori_loop(0, FIELDS, one_field, 0)
-
-    def row_ghosts(side):
-        def put(f, found):
-            row_in[side, f] = found
-
-        two = [wanted[0, 0, :, pl.ds(256 * side + 128 * r, 128)] for r in range(2)]
-        ghosts(jnp.where(sub8 < 4, two[0], two[1]), put)
-
-    def column_ghosts(side):
-        def put(f, found):
-            own = jnp.where(lane8 // CT == lax.rem(sub8, 4), found, 0.0)
-            col_in[side, f, pl.ds(0, 1), :] = jnp.sum(own[0:4], axis=0, keepdims=True)
-            col_in[side, f, pl.ds(1, 1), :] = jnp.sum(own[4:8], axis=0, keepdims=True)
-
-        line = jnp.broadcast_to(wanted[0, 0, :, pl.ds(512, 128)], (8, 128))
-        ghosts(lanes_at(line, 64 * side + 2 * lax.rem(lane8, CT) + sub8 // 4), put)
-
     pl.when(left)(to_right.wait_recv)
     pl.when(right)(to_left.wait_recv)
     pl.when(left & right)(add_columns)
@@ -338,34 +416,84 @@
     @pl.when(up)
     def _():
         to_down.wait_recv()
-        add_rows(0)
+        add_rows(0, row_in.at[0])
 
     @pl.when(down)
     def _():
         to_up.wait_recv()
-        add_rows(1)
-
-    @pl.when(edge)
-    def _():
-        for j in range(9):
-            slot_copies[8 - j].wait_recv()
-
-    pl.when(l == 0)(lambda: column_ghosts(0))
-    pl.when(l == nl - 1)(lambda: column_ghosts(1))
-    pl.when((l == 0) | (l == nl - 1))(add_columns)
-
-    @pl.when(c == 0)
-    def _():
-        row_ghosts(0)
-        add_rows(0)
-
-    @pl.when(c == nc - 1)
-    def _():
-        row_ghosts(1)
-        add_rows(1)
-
-    for copy, (la, ca) in zip(slot_copies, others):
-        pl.when(on_edge(la, ca))(copy.wait_send)
+        add_rows(1, row_in.at[1])
+
+    def name_row(side):
+        two = [wanted[0, 0, :, pl.ds(256 * side + 128 * r, 128)] for r in range(2)]
+        named[0] = jnp.where(sub8 < 4, two[0], two[1])
+
+    def name_column(side):
+        line = jnp.broadcast_to(wanted[0, 0, :, pl.ds(512, 128)], (8, 128))
+        named[1] = lanes_at(line, 64 * side + 2 * lax.rem(lane8, CT) + sub8 // 4)
+
+    pl.when(c == 0)(lambda: name_row(0))
+    pl.when(c == nc - 1)(lambda: name_row(1))
+    pl.when(l == 0)(lambda: name_column(0))
+    pl.when(l == nl - 1)(lambda: name_column(1))
+
+    def pick_ghosts(kind, group, fresh):
+        index = named[kind]
+        owner = index // SLOTS
+        lane = lax.rem(index, SLOTS)
+        three = range(3 * group, 3 * group + 3)
+        here = [owner == others[j][0] * nc + others[j][1] for j in three]
+
+        def one_field(f, _):
+            found = jnp.zeros((8, 128), jnp.float32) if fresh else picked[kind, f]
+            for mine, j in zip(here, three):
+                half = slots_in[j, f]
+                found = jnp.where(mine, lanes_at(jnp.concatenate([half, half], axis=0), lane), found)
+            picked[kind, f] = found
+            return 0
+
+        lax.fori_loop(0, FIELDS, one_field, 0)
+
+    pass_on = [
+        remote(slots_in.at[3:6], slots_in.at[6:9], 13, p, l - 1, c),
+        remote(slots_in.at[3:6], slots_in.at[0:3], 14, p, l + 1, c),
+    ]
+    to_mate = [
+        remote(slots_in.at[3 * group : 3 * group + 2], slots_in.at[3 * group + 1 : 3 * group + 3], 15 + group, p, l, c - 1)
+        for group in range(3)
+    ]
+    for turn, group in enumerate((1, 0, 2)):
+        for j in range(3 * group, 3 * group + 3):
+            pl.when(direct_in[j])(slot_copies[8 - j].wait_recv)
+        if group == 0:
+            pl.when(take_left)(pass_on[1].wait_recv)
+        if group == 1:
+            pl.when(pass_left)(pass_on[0].start)
+            pl.when(pass_right)(pass_on[1].start)
+        if group == 2:
+            pl.when(take_right)(pass_on[0].wait_recv)
+        pl.when(mate_gives)(to_mate[group].start)
+        pl.when(mate_takes)(to_mate[group].wait_recv)
+        pl.when(row_edge)(lambda: pick_ghosts(0, group, turn == 0))
+        pl.when(at_end)(lambda: pick_ghosts(1, group, turn == 0))
+
+    @pl.when(at_end)
+    def _():
+        side = jnp.where(l == 0, 0, 1)
+        for f in range(FIELDS):
+            own = jnp.where(lane8 // CT == lax.rem(sub8, 4), picked[1, f], 0.0)
+            col_in[side, f, pl.ds(0, 1), :] = jnp.sum(own[0:4], axis=0, keepdims=True)
+            col_in[side, f, pl.ds(1, 1), :] = jnp.sum(own[4:8], axis=0, keepdims=True)
+        add_columns()
+
+    pl.when(c == 0)(lambda: add_rows(0, picked.at[0]))
+    pl.when(c == nc - 1)(lambda: add_rows(1, picked.at[0]))
+
+    for j in range(9):
+        pl.when(flows_out[j])(slot_copies[j].wait_send)
+    pl.when(pass_left)(pass_on[0].wait_send)
+    pl.when(pass_right)(pass_on[1].wait_send)
+    for copy in to_mate:
+        pl.when(mate_gives)(copy.wait_send)
     pl.when(left)(to_left.wait_send)
     pl.when(right)(to_right.wait_send)
     pl.when(up)(to_up.wait_send)
@@ -394,9 +522,12 @@
             pltpu.VMEM((FIELDS, TALL, CP), f32),
             pltpu.VMEM((FIELDS, TALL, CP), f32),
             pltpu.VMEM((FIELDS, TALL, CP), f32),
+            pltpu.VMEM((2, FIELDS, 8, CP), f32),
+            pltpu.VMEM((2, 8, CP), i32),
             pltpu.SemaphoreType.DMA((12,)),
-            pltpu.SemaphoreType.DMA((13,)),
-            pltpu.SemaphoreType.DMA((13,)),
+            pltpu.SemaphoreType.DMA((18,)),
+            pltpu.SemaphoreType.DMA((18,)),
+            pltpu.SemaphoreType.REGULAR,
         ],
         compiler_params=pltpu.CompilerParams(
             collective_id=0, has_side_effects=True, vmem_limit_bytes=32 * 1024 * 1024

time: 28.3 us -> 25.3 us (0.89)
  the two profiles are of different devices: /device:TPU:1 before, /device:TPU:248 now
where the time goes in v3:
time: 25.3 us; the launch traced here: 25.1 us
  Pallas kernels  24.3 us (96%)
  local copies, waits for them, and re-layouts  0.8 us (3%)
    pallas_call x1, Pallas kernels, body(): pl.pallas_call(kernel, out_shape=pltpu.VMEM((FIELDS, TALL, CP), f32), in_...  24.3 us
    unnamed x1, local copies, waits for them, and re-layouts  0.8 us

profile of v3, /device:TPU:248, one launch (start us, length us, event | category | flops | bytes accessed | tf_op | source)
XLA Modules:
  0.0 25.1 jit_solution(12880354716818025975)
XLA Ops:
  0.0 24.3 %shard_map.55 = f32[8,128,128]{2,1,0:T(8,128)S(1)} custom-call(f32[8,128,128]{2,1,0:T(8,128)} %bitcast.3, s32[1,1,1,128]{3,2,1,0:T(1,128)} %row_hbm.1, s32[1,1,1,128]{3,2,1,0:T(1,128)} %col_hbm.1, f32[1,1,1,4,128]{4,3,2,1,0:T(4,128)} %weight_hbm.1, s32[1,1,1,640]{3,2,1,0:T(1,128)} %ghost_hbm.1), custom_call_target="tpu_custom_call" | custom-call | tf_op jit(solution)/shard_map/pallas_call | solution.py:505
  24.3 0.8 %copy.7 = f32[1,8,4,32,128]{4,3,2,1,0:T(8,128)} copy(f32[1,8,4,32,128]{4,3,2,1,0:T(8,128)S(1)} %bitcast.2) | data formatting | bytes 1048576

commit v4 on v3

--- a/solution.py
+++ b/solution.py
@@ -22,6 +22,7 @@
 MESH = pl.DeviceIdType.MESH
 RUN = 8
 AROUND = [(dl, dc) for dl in (-1, 0, 1) for dc in (-1, 0, 1)]
+SEND_ORDER = (2, 1, 0, 5, 4, 3, 8, 7, 6)
 TURNED = [(0, 1.0), (1, -1.0), (3, 1.0), (2, 1.0), (4, -1.0), (6, 1.0), (5, 1.0), (7, 1.0)]
 
 
@@ -93,10 +94,11 @@
     edge = on_edge(l, c)
     others = [(wrap(l + dl, nl), wrap(c + dc, nc)) for dl, dc in AROUND]
 
-    late = 4
+    late_left, late_right = 4, 4
     place = lax.rem(l, RUN)
 
     def passed(panel, tile, la):
+        late = jnp.where(la < tile, late_left, late_right)
         far = (panel == 1) | ((lax.rem(tile, RUN) >= late) & (lax.rem(la, RUN) != RUN - 1))
         return far & (tile // RUN == la // RUN)
 
@@ -129,7 +131,7 @@
     helped_0 = (p == 0) & (place == RUN - 1) & (beside | at_end)
     at_helper = (c == 2) | (c == nc - 3)
     helper_1 = (p == 1) & at_seam & ~at_end & at_helper
-    helper_0 = (p == 0) & (place == RUN - 1) & ~at_end & at_helper
+    helper_0 = (p == 0) & (place == RUN - 2) & (l != nl - 2) & at_helper
     end_helper = (l == nl - 2) & ~beside
     over_left, over_right = left & (place == 0), right & (place == RUN - 1)
     seam_by_help = helped_1 & ~at_end
@@ -142,7 +144,7 @@
 
     for j, (la, ca) in enumerate(others):
         by_help = (p == 1) & (lax.rem(la, RUN) == RUN - 1)
-        to_l = jnp.where(by_help & (la == nl - 1), nl - 2, la)
+        to_l = jnp.where(by_help, la - 1, la)
         to_c = jnp.where(by_help, jnp.clip(ca, 2, nc - 3), ca)
         pl.when(direct_in[j] & ~shut_in[j])(lambda: greet(1 - p, to_l, to_c))
 
@@ -153,7 +155,7 @@
 
     @pl.when(helped_0 | helped_1)
     def _():
-        greet(p, jnp.where(at_end, nl - 2, l), inner)
+        greet(p, jnp.where(at_end, nl - 2, jnp.where(p == 0, l - 1, l)), inner)
         pl.when(seam_by_help)(lambda: greet(p, jnp.where(place == 0, l - 1, l + 1), inner))
 
     @pl.when((p == 0) & (l < nl - 1) & row_edge & (place >= RUN - 2))
@@ -187,13 +189,29 @@
     on_left = jnp.where(first, w[0:1], jnp.where(second, w[2:3], 0.0))
     on_right = jnp.where(first, w[1:2], jnp.where(second, w[3:4], 0.0))
     pick = jnp.broadcast_to(cols[0, 0], (CT, CP))
+    pick_next = pick + 1
+    halves = [(h, lax.rem(sub8 // h, 2) == 0) for h in (4, 2)]
+
+    def fold(a, b, step):
+        h, low = halves[step]
+        if h == 4:
+            return jnp.where(low, a, b) + pltpu.roll(jnp.where(low, b, a), 4, 0)
+        return jnp.where(low, a + pltpu.roll(a, 6, 0), b + pltpu.roll(b, 2, 0))
+
     for f in range(FIELDS):
         large[f].wait()
         target, sign = TURNED[f]
+        sums = []
         for k in range(SHELLS):
             plane = x[f, CT * k : CT * (k + 1), :]
-            mixed = on_left * lanes_at(plane, pick) + on_right * lanes_at(plane, pick + 1)
-            slots[target, k : k + 1, :] = sign * jnp.sum(mixed, axis=0, keepdims=True)
+            mixed = on_left * lanes_at(plane, pick) + on_right * lanes_at(plane, pick_next)
+            sums.append((mixed[0:8] + mixed[8:16]) + (mixed[16:24] + mixed[24:32]))
+        four = fold(fold(sums[0], sums[2], 0), fold(sums[1], sums[3], 0), 1)
+        both = four + pltpu.roll(four, 7, 0)
+        for k in range(SHELLS):
+            line = both[2 * k : 2 * k + 1]
+            at = SHELLS * target + k
+            slots[at : at + 1, :] = line if sign > 0 else -line
 
     def one(flag):
         return flag.astype(jnp.int32)
@@ -222,7 +240,8 @@
     ]
 
     def send_slots(wave):
-        for j, (la, ca) in enumerate(others):
+        for j in SEND_ORDER:
+            la, ca = others[j]
             spot = lax.rem(la, RUN)
             turn = jnp.where(p == 0, 0, jnp.where(spot == 0, 0, jnp.where(spot < 3, 0, jnp.where(spot < 5, 0, 0))))
             pl.when(flows_out[j] & ~shut_out[j] & ~helped_0 & (turn == wave))(slot_copies[j].start)
@@ -235,8 +254,8 @@
     @pl.when(helper_0 | helper_1)
     def _():
         first = jnp.where(c == 2, 0, nc - 2)
-        tell(p, l, first)
-        tell(p, l, first + 1)
+        for more in range(2):
+            tell(p, jnp.where(p == 0, l + 1, l), first + more)
 
     @pl.when(end_helper)
     def _():
@@ -352,7 +371,7 @@
         pl.semaphore_wait(told, 1)
         pl.when(over_left & seam_by_help)(to_left.start)
         pl.when(over_right & seam_by_help)(to_right.start)
-        for j in range(9):
+        for j in SEND_ORDER:
             pl.when(flows_out[j] & (shut_out[j] | helped_0))(slot_copies[j].start)
 
     def near(n):
@@ -362,44 +381,49 @@
     inverse_r = 1.0 / ((1.0 - (SHELLS - 1 - shell8) * RADIAL_STEP) * ht)
     upper = sub8 < 4
 
-    def add_rows(side, rim):
-        u = [rim[f] for f in range(FIELDS)]
-        terms = cell_terms(u)
-        if side == 0:
-            jobs = ((0, -near(2), -near(1)), (1, 0.0, -near(2)))
-        else:
-            jobs = ((CT - 1, near(1), near(2)), (CT - 2, near(2), 0.0))
+    row_jobs = []
+    for jobs in (
+        ((0, -near(2), -near(1)), (1, 0.0, -near(2))),
+        ((CT - 1, near(1), near(2)), (CT - 2, near(2), 0.0)),
+    ):
+        row_jobs.append([])
         for row, one_w, two_w in jobs:
             th = angle_t(jnp.full((8, 128), row, jnp.float32))
             s8, c8 = jnp.sin(th), jnp.cos(th)
-            scale = jnp.where(upper, one_w, two_w) * inverse_r
+            row_jobs[-1].append((row, jnp.where(upper, one_w, two_w) * inverse_r, (c8 * cf, c8 * sf, -s8)))
+
+    def add_rows(side, fields):
+        terms = cell_terms(fields)
+        for row, scale, e in row_jobs[side]:
             where = pl.ds(row, SHELLS, stride=CT)
-            for f, value in enumerate(flux_along(terms, (c8 * cf, c8 * sf, -s8))):
+            for f, value in enumerate(flux_along(terms, e)):
                 value = value * scale
                 acc[f, where, :] = acc[f, where, :] - (value[0:4] + value[4:8])
 
     rim = (lanes < 2) | (lanes >= CP - 2)
 
+    sub4 = lax.broadcasted_iota(jnp.int32, (4, 128), 0)
+    lane4 = lax.broadcasted_iota(jnp.int32, (4, 128), 1)
+    th = angle_t(lax.rem(lane4, CT).astype(jnp.float32))
+    shell4 = (lane4 // CT).astype(jnp.float32)
+    share = 1.0 / ((1.0 - (SHELLS - 1 - shell4) * RADIAL_STEP) * jnp.sin(th) * hp)
+    column_jobs = []
+    for from_left, from_right, weights in (
+        (0, CP - 1, (-near(2), -near(1), near(1), near(2))),
+        (1, CP - 2, (0.0, -near(2), near(2), 0.0)),
+    ):
+        ph = angle_f(jnp.where(sub4 < 2, from_left, from_right).astype(jnp.float32))
+        scale = jnp.where(
+            sub4 < 2,
+            jnp.where(sub4 == 0, weights[0], weights[1]),
+            jnp.where(sub4 == 2, weights[2], weights[3]),
+        ) * share
+        column_jobs.append((scale, (-jnp.sin(ph), jnp.cos(ph), None)))
+
     def add_columns():
-        sub4 = lax.broadcasted_iota(jnp.int32, (4, 128), 0)
-        lane4 = lax.broadcasted_iota(jnp.int32, (4, 128), 1)
         u = [jnp.concatenate([col_in[0, f], col_in[1, f]], axis=0) for f in range(FIELDS)]
         terms = cell_terms(u)
-        th = angle_t(lax.rem(lane4, CT).astype(jnp.float32))
-        shell4 = (lane4 // CT).astype(jnp.float32)
-        share = 1.0 / ((1.0 - (SHELLS - 1 - shell4) * RADIAL_STEP) * jnp.sin(th) * hp)
-        parts = []
-        for from_left, from_right, weights in (
-            (0, CP - 1, (-near(2), -near(1), near(1), near(2))),
-            (1, CP - 2, (0.0, -near(2), near(2), 0.0)),
-        ):
-            ph = angle_f(jnp.where(sub4 < 2, from_left, from_right).astype(jnp.float32))
-            scale = jnp.where(
-                sub4 < 2,
-                jnp.where(sub4 == 0, weights[0], weights[1]),
-                jnp.where(sub4 == 2, weights[2], weights[3]),
-            ) * share
-            parts.append([v * scale for v in flux_along(terms, (-jnp.sin(ph), jnp.cos(ph), None))])
+        parts = [[v * scale for v in flux_along(terms, e)] for scale, e in column_jobs]
         lines = []
         for f in range(FIELDS):
             close, far = parts[0][f], parts[1][f]
@@ -416,20 +440,23 @@
     @pl.when(up)
     def _():
         to_down.wait_recv()
-        add_rows(0, row_in.at[0])
+        add_rows(0, [row_in[0, f] for f in range(FIELDS)])
 
     @pl.when(down)
     def _():
         to_up.wait_recv()
-        add_rows(1, row_in.at[1])
+        add_rows(1, [row_in[1, f] for f in range(FIELDS)])
+
+    def name(kind, lines):
+        for r, line in enumerate(lines):
+            named[kind, r] = line
 
     def name_row(side):
-        two = [wanted[0, 0, :, pl.ds(256 * side + 128 * r, 128)] for r in range(2)]
-        named[0] = jnp.where(sub8 < 4, two[0], two[1])
+        name(0, [jnp.broadcast_to(wanted[0, 0, :, pl.ds(256 * side + 128 * r, 128)], (8, 128)) for r in range(2)])
 
     def name_column(side):
         line = jnp.broadcast_to(wanted[0, 0, :, pl.ds(512, 128)], (8, 128))
-        named[1] = lanes_at(line, 64 * side + 2 * lax.rem(lane8, CT) + sub8 // 4)
+        name(1, [lanes_at(line, 64 * side + 2 * lax.rem(lane8, CT) + r) for r in range(2)])
 
     pl.when(c == 0)(lambda: name_row(0))
     pl.when(c == nc - 1)(lambda: name_row(1))
@@ -437,21 +464,18 @@
     pl.when(l == nl - 1)(lambda: name_column(1))
 
     def pick_ghosts(kind, group, fresh):
-        index = named[kind]
-        owner = index // SLOTS
-        lane = lax.rem(index, SLOTS)
-        three = range(3 * group, 3 * group + 3)
-        here = [owner == others[j][0] * nc + others[j][1] for j in three]
-
-        def one_field(f, _):
-            found = jnp.zeros((8, 128), jnp.float32) if fresh else picked[kind, f]
-            for mine, j in zip(here, three):
-                half = slots_in[j, f]
-                found = jnp.where(mine, lanes_at(jnp.concatenate([half, half], axis=0), lane), found)
-            picked[kind, f] = found
-            return 0
-
-        lax.fori_loop(0, FIELDS, one_field, 0)
+        for r in range(2):
+            index = named[kind, r]
+            owner = index // SLOTS
+            lane = lax.rem(index, SLOTS)
+            found = [None if fresh else picked[kind, r, 8 * m : 8 * m + 8, :] for m in range(4)]
+            for j in range(3 * group, 3 * group + 3):
+                here = owner == others[j][0] * nc + others[j][1]
+                for m in range(4):
+                    value = lanes_at(slots_in[j, 8 * m : 8 * m + 8, :], lane)
+                    found[m] = value if found[m] is None else jnp.where(here, value, found[m])
+            for m in range(4):
+                picked[kind, r, 8 * m : 8 * m + 8, :] = found[m]
 
     pass_on = [
         remote(slots_in.at[3:6], slots_in.at[6:9], 13, p, l - 1, c),
@@ -479,14 +503,25 @@
     @pl.when(at_end)
     def _():
         side = jnp.where(l == 0, 0, 1)
-        for f in range(FIELDS):
-            own = jnp.where(lane8 // CT == lax.rem(sub8, 4), picked[1, f], 0.0)
-            col_in[side, f, pl.ds(0, 1), :] = jnp.sum(own[0:4], axis=0, keepdims=True)
-            col_in[side, f, pl.ds(1, 1), :] = jnp.sum(own[4:8], axis=0, keepdims=True)
+        mine = lane8 // CT == lax.rem(sub8, 4)
+        for r in range(2):
+            for m in range(4):
+                own = jnp.where(mine, picked[1, r, 8 * m : 8 * m + 8, :], 0.0)
+                own = own + pltpu.roll(own, 7, 0)
+                own = own + pltpu.roll(own, 6, 0)
+                col_in[side, 2 * m, r : r + 1, :] = own[0:1]
+                col_in[side, 2 * m + 1, r : r + 1, :] = own[4:5]
         add_columns()
 
-    pl.when(c == 0)(lambda: add_rows(0, picked.at[0]))
-    pl.when(c == nc - 1)(lambda: add_rows(1, picked.at[0]))
+    def add_ghost_rows(side):
+        fields = [
+            jnp.concatenate([picked[0, r, SHELLS * f : SHELLS * f + SHELLS, :] for r in range(2)], axis=0)
+            for f in range(FIELDS)
+        ]
+        add_rows(side, fields)
+
+    pl.when(c == 0)(lambda: add_ghost_rows(0))
+    pl.when(c == nc - 1)(lambda: add_ghost_rows(1))
 
     for j in range(9):
         pl.when(flows_out[j])(slot_copies[j].wait_send)
@@ -513,8 +548,8 @@
             pltpu.VMEM((1, 1, 1, SLOTS), i32),
             pltpu.VMEM((1, 1, 1, 4, SLOTS), f32),
             pltpu.VMEM((1, 1, 1, 640), i32),
-            pltpu.VMEM((FIELDS, SHELLS, SLOTS), f32),
-            pltpu.VMEM((9, FIELDS, SHELLS, SLOTS), f32),
+            pltpu.VMEM((FIELDS * SHELLS, SLOTS), f32),
+            pltpu.VMEM((9, FIELDS * SHELLS, SLOTS), f32),
             pltpu.VMEM((2, FIELDS, 8, CP), f32),
             pltpu.VMEM((2, FIELDS, 8, CP), f32),
             pltpu.VMEM((2, FIELDS, 2, TALL), f32),
@@ -522,8 +557,8 @@
             pltpu.VMEM((FIELDS, TALL, CP), f32),
             pltpu.VMEM((FIELDS, TALL, CP), f32),
             pltpu.VMEM((FIELDS, TALL, CP), f32),
-            pltpu.VMEM((2, FIELDS, 8, CP), f32),
-            pltpu.VMEM((2, 8, CP), i32),
+            pltpu.VMEM((2, 2, FIELDS * SHELLS, CP), f32),
+            pltpu.VMEM((2, 2, 8, CP), i32),
             pltpu.SemaphoreType.DMA((12,)),
             pltpu.SemaphoreType.DMA((18,)),
             pltpu.SemaphoreType.DMA((18,)),

time: 25.3 us -> 24 us (0.949)
  the two profiles are of different devices: /device:TPU:248 before, /device:TPU:184 now
where the time goes in v4:
time: 24 us; the launch traced here: 23.9 us
  Pallas kernels  23.1 us (96%)
  local copies, waits for them, and re-layouts  0.8 us (3%)
    pallas_call x1, Pallas kernels, body(): pl.pallas_call(kernel, out_shape=pltpu.VMEM((FIELDS, TALL, CP), f32), in_...  23.1 us
    unnamed x1, local copies, waits for them, and re-layouts  0.8 us

profile of v4, /device:TPU:184, one launch (start us, length us, event | category | flops | bytes accessed | tf_op | source)
XLA Modules:
  0.0 23.9 jit_solution(8004447923733521424)
XLA Ops:
  0.0 23.1 %shard_map.55 = f32[8,128,128]{2,1,0:T(8,128)S(1)} custom-call(f32[8,128,128]{2,1,0:T(8,128)} %bitcast.3, s32[1,1,1,128]{3,2,1,0:T(1,128)} %row_hbm.1, s32[1,1,1,128]{3,2,1,0:T(1,128)} %col_hbm.1, f32[1,1,1,4,128]{4,3,2,1,0:T(4,128)} %weight_hbm.1, s32[1,1,1,640]{3,2,1,0:T(1,128)} %ghost_hbm.1), custom_call_target="tpu_custom_call" | custom-call | tf_op jit(solution)/shard_map/pallas_call | solution.py:540
  23.1 0.8 %copy.7 = f32[1,8,4,32,128]{4,3,2,1,0:T(8,128)} copy(f32[1,8,4,32,128]{4,3,2,1,0:T(8,128)S(1)} %bitcast.2) | data formatting | bytes 1048576

commit v5 on v4

--- a/solution.py
+++ b/solution.py
@@ -81,12 +81,15 @@
         return (la == 0) | (la == nl - 1) | on_row(ca)
 
     small = [
-        pltpu.make_async_copy(src, dst, in_sem.at[FIELDS + i])
+        pltpu.make_async_copy(src, dst, in_sem.at[2 + i])
         for i, (src, dst) in enumerate(
             ((row_hbm, rows), (col_hbm, cols), (weight_hbm, weight), (ghost_hbm, wanted))
         )
     ]
-    large = [pltpu.make_async_copy(x_hbm.at[f], x.at[f], in_sem.at[f]) for f in range(FIELDS)]
+    half = FIELDS // 2
+    large = [
+        pltpu.make_async_copy(x_hbm.at[half * i : half * (i + 1)], x.at[half * i : half * (i + 1)], in_sem.at[i]) for i in range(2)
+    ]
     for load in small + large:
         load.start()
 
@@ -103,6 +106,7 @@
         return far & (tile // RUN == la // RUN)
 
     flows_out, direct_in, shut_out, shut_in = [], [], [], []
+    beside = (c < 2) | (c >= nc - 2)
     to_panel_1 = p == 0
     for (la, ca), (dl, dc) in zip(others, AROUND):
         flow, got = on_edge(la, ca), edge
@@ -115,10 +119,15 @@
             got = got & ~((p == 0) & (l == 0) & (lax.rem(c, 2) == 0))
         flows_out.append(flow)
         direct_in.append(got)
-        shut_out.append((p == 1) & (((place == RUN - 1) & (dl <= 0)) | ((place == 0) & (dl == -1))))
-        shut_in.append((p == 0) & (((place == RUN - 1) & (dl >= 0)) | ((place == RUN - 2) & (dl == 1))))
+        shut = ((place == RUN - 1) & (dl <= 0)) | ((place == 0) & (dl == -1))
+        if dl == 1:
+            shut = shut | ((l == nl - 2) & beside)
+        shut_out.append((p == 1) & shut)
+        shut = ((place == RUN - 1) & (dl >= 0)) | ((place == RUN - 2) & (dl == 1))
+        if dl == -1:
+            shut = shut | ((l == nl - 1) & ((ca < 2) | (ca >= nc - 2)))
+        shut_in.append((p == 0) & shut)
     row_edge = on_row(c)
-    take_left, take_right = row_edge & left & passed(p, l, l - 1), row_edge & right & passed(p, l, l + 1)
     pass_left, pass_right = row_edge & left & passed(p, l - 1, l), row_edge & right & passed(p, l + 1, l)
     mate_gives = (p == 0) & (l == 0) & (lax.rem(c, 2) == 1)
     mate_takes = (p == 0) & (l == 0) & (lax.rem(c, 2) == 0)
@@ -126,15 +135,14 @@
     inner = jnp.clip(c, 2, nc - 3)
     at_seam = (place == 0) | (place == RUN - 1)
     at_end = (l == 0) | (l == nl - 1)
-    beside = (c < 2) | (c >= nc - 2)
-    helped_1 = (p == 1) & at_seam & (beside | at_end)
+    helped_1 = (p == 1) & ((at_seam & (beside | at_end)) | ((l == nl - 2) & beside))
     helped_0 = (p == 0) & (place == RUN - 1) & (beside | at_end)
     at_helper = (c == 2) | (c == nc - 3)
     helper_1 = (p == 1) & at_seam & ~at_end & at_helper
     helper_0 = (p == 0) & (place == RUN - 2) & (l != nl - 2) & at_helper
     end_helper = (l == nl - 2) & ~beside
     over_left, over_right = left & (place == 0), right & (place == RUN - 1)
-    seam_by_help = helped_1 & ~at_end
+    seam_by_help = helped_1 & at_seam & ~at_end
     near_left, near_right = left & ~(over_left & seam_by_help), right & ~(over_right & seam_by_help)
 
     barrier = pltpu.get_barrier_semaphore()
@@ -199,7 +207,8 @@
         return jnp.where(low, a + pltpu.roll(a, 6, 0), b + pltpu.roll(b, 2, 0))
 
     for f in range(FIELDS):
-        large[f].wait()
+        if f % half == 0:
+            large[f // half].wait()
         target, sign = TURNED[f]
         sums = []
         for k in range(SHELLS):
@@ -221,23 +230,22 @@
         expected = expected + one(flow & ~shut & ~helped_0)
     expected = expected + one(helper_1) * (6 + 2 * one(place == RUN - 1)) + 8 * one(helper_0)
     served = jnp.where(at_helper, 3, 1)
-    at_panel_1 = 2 * served + jnp.where(at_helper, 7, 3)
+    at_panel_1 = 2 * served + jnp.where(at_helper, 9, 3)
     expected = expected + one(end_helper) * jnp.where(p == 1, at_panel_1, 7 * served)
     pl.semaphore_wait(barrier, expected)
 
-    def remote(src, dst, i, *device):
+    def remote(src, dst, sent, arrived, *device):
         return pltpu.make_async_remote_copy(
-            src_ref=src, dst_ref=dst, send_sem=send_sem.at[i], recv_sem=recv_sem.at[i],
+            src_ref=src, dst_ref=dst, send_sem=send_sem.at[sent], recv_sem=recv_sem.at[arrived],
             device_id=device, device_id_type=MESH,
         )
 
     slot_copies = [
-        pltpu.make_async_remote_copy(
-            src_ref=slots, dst_ref=slots_in.at[8 - j], send_sem=send_sem.at[j], recv_sem=recv_sem.at[8 - j],
-            device_id=(1 - p, la, ca), device_id_type=MESH,
-        )
-        for j, (la, ca) in enumerate(others)
+        remote(slots, slots_in.at[8 - j], 0, (8 - j) // 3, 1 - p, la, ca) for j, (la, ca) in enumerate(others)
     ]
+
+    def whole(sent, arrived, sets):
+        return remote(sets, sets, sent, arrived, 1 - p, l, c)
 
     def send_slots(wave):
         for j in SEND_ORDER:
@@ -268,6 +276,7 @@
             for more in range(2):
                 tell(p, nl - 1, first + more)
                 pl.when(p == 1)(lambda: tell(p, 0, first + more))
+                pl.when(p == 1)(lambda: tell(p, nl - 2, first + more))
 
     lanes = lax.broadcasted_iota(jnp.int32, (TALL, CP), 1)
     packed = jnp.zeros((TALL, CP), jnp.float32)
@@ -282,10 +291,10 @@
         col_out[1, f] = upright[4 * f : 4 * f + 2]
         col_out[0, f] = upright[4 * f + 2 : 4 * f + 4]
 
-    to_up = remote(row_out.at[0], row_in.at[1], 9, p, l, c - 1)
-    to_down = remote(row_out.at[1], row_in.at[0], 10, p, l, c + 1)
-    to_left = remote(col_out.at[0], col_in.at[1], 11, p, l - 1, c)
-    to_right = remote(col_out.at[1], col_in.at[0], 12, p, l + 1, c)
+    to_up = remote(row_out.at[0], row_in.at[1], 1, 4, p, l, c - 1)
+    to_down = remote(row_out.at[1], row_in.at[0], 1, 3, p, l, c + 1)
+    to_left = remote(col_out.at[0], col_in.at[1], 2, 6, p, l - 1, c)
+    to_right = remote(col_out.at[1], col_in.at[0], 2, 5, p, l + 1, c)
     pl.when(near_left)(to_left.start)
     pl.when(near_right)(to_right.start)
     pl.when(up)(to_up.start)
@@ -478,25 +487,19 @@
                 picked[kind, r, 8 * m : 8 * m + 8, :] = found[m]
 
     pass_on = [
-        remote(slots_in.at[3:6], slots_in.at[6:9], 13, p, l - 1, c),
-        remote(slots_in.at[3:6], slots_in.at[0:3], 14, p, l + 1, c),
+        remote(slots_in.at[3:6], slots_in.at[6:9], 3, 2, p, l - 1, c),
+        remote(slots_in.at[3:6], slots_in.at[0:3], 3, 0, p, l + 1, c),
     ]
     to_mate = [
-        remote(slots_in.at[3 * group : 3 * group + 2], slots_in.at[3 * group + 1 : 3 * group + 3], 15 + group, p, l, c - 1)
+        remote(slots_in.at[3 * group : 3 * group + 2], slots_in.at[3 * group + 1 : 3 * group + 3], 4, group, p, l, c - 1)
         for group in range(3)
     ]
     for turn, group in enumerate((1, 0, 2)):
-        for j in range(3 * group, 3 * group + 3):
-            pl.when(direct_in[j])(slot_copies[8 - j].wait_recv)
-        if group == 0:
-            pl.when(take_left)(pass_on[1].wait_recv)
+        pl.when(edge)(whole(0, group, slots_in.at[3 * group : 3 * group + 3]).wait_recv)
         if group == 1:
             pl.when(pass_left)(pass_on[0].start)
             pl.when(pass_right)(pass_on[1].start)
-        if group == 2:
-            pl.when(take_right)(pass_on[0].wait_recv)
         pl.when(mate_gives)(to_mate[group].start)
-        pl.when(mate_takes)(to_mate[group].wait_recv)
         pl.when(row_edge)(lambda: pick_ghosts(0, group, turn == 0))
         pl.when(at_end)(lambda: pick_ghosts(1, group, turn == 0))
 
@@ -523,16 +526,18 @@
     pl.when(c == 0)(lambda: add_ghost_rows(0))
     pl.when(c == nc - 1)(lambda: add_ghost_rows(1))
 
-    for j in range(9):
-        pl.when(flows_out[j])(slot_copies[j].wait_send)
-    pl.when(pass_left)(pass_on[0].wait_send)
-    pl.when(pass_right)(pass_on[1].wait_send)
-    for copy in to_mate:
-        pl.when(mate_gives)(copy.wait_send)
-    pl.when(left)(to_left.wait_send)
-    pl.when(right)(to_right.wait_send)
-    pl.when(up)(to_up.wait_send)
-    pl.when(down)(to_down.wait_send)
+    def wait_sent(sent, number, sets):
+        for n in range(1, len(sets) + 1):
+            pl.when(number == n)(whole(sent, 0, sets[n - 1]).wait_send)
+
+    number = 0
+    for flow in flows_out:
+        number = number + one(flow)
+    wait_sent(0, number, [slots_in.at[0:n] for n in range(1, 10)])
+    wait_sent(1, one(up) + one(down), [row_in.at[0:n] for n in (1, 2)])
+    wait_sent(2, one(left) + one(right), [col_in.at[0:n] for n in (1, 2)])
+    wait_sent(3, one(pass_left) + one(pass_right), [slots_in.at[0:n] for n in (3, 6)])
+    pl.when(mate_gives)(whole(4, 0, slots_in.at[0:6]).wait_send)
 
 
 def body(state_now, send_row, send_col, send_weight, ghost_slot):
@@ -559,9 +564,9 @@
             pltpu.VMEM((FIELDS, TALL, CP), f32),
             pltpu.VMEM((2, 2, FIELDS * SHELLS, CP), f32),
             pltpu.VMEM((2, 2, 8, CP), i32),
-            pltpu.SemaphoreType.DMA((12,)),
-            pltpu.SemaphoreType.DMA((18,)),
-            pltpu.SemaphoreType.DMA((18,)),
+            pltpu.SemaphoreType.DMA((6,)),
+            pltpu.SemaphoreType.DMA((5,)),
+            pltpu.SemaphoreType.DMA((7,)),
             pltpu.SemaphoreType.REGULAR,
         ],
         compiler_params=pltpu.CompilerParams(

time: 24 us -> 22.9 us (0.954)
  the two profiles are of different devices: /device:TPU:184 before, /device:TPU:32 now
where the time goes in v5:
time: 22.9 us; the launch traced here: 22.8 us
  Pallas kernels  22 us (96%)
  local copies, waits for them, and re-layouts  0.8 us (3%)
    pallas_call x1, Pallas kernels, body(): pl.pallas_call(kernel, out_shape=pltpu.VMEM((FIELDS, TALL, CP), f32), in_...  22 us
    unnamed x1, local copies, waits for them, and re-layouts  0.8 us

profile of v5, /device:TPU:32, one launch (start us, length us, event | category | flops | bytes accessed | tf_op | source)
XLA Modules:
  0.0 22.8 jit_solution(7377830484199047119)
XLA Ops:
  0.0 22.0 %shard_map.55 = f32[8,128,128]{2,1,0:T(8,128)S(1)} custom-call(f32[8,128,128]{2,1,0:T(8,128)} %bitcast.3, s32[1,1,1,128]{3,2,1,0:T(1,128)} %row_hbm.1, s32[1,1,1,128]{3,2,1,0:T(1,128)} %col_hbm.1, f32[1,1,1,4,128]{4,3,2,1,0:T(4,128)} %weight_hbm.1, s32[1,1,1,640]{3,2,1,0:T(1,128)} %ghost_hbm.1), custom_call_target="tpu_custom_call" | custom-call | tf_op jit(solution)/shard_map/pallas_call | solution.py:545
  22.0 0.8 %copy.7 = f32[1,8,4,32,128]{4,3,2,1,0:T(8,128)} copy(f32[1,8,4,32,128]{4,3,2,1,0:T(8,128)S(1)} %bitcast.2) | data formatting | bytes 1048576

commit v6 on v5

--- a/solution.py
+++ b/solution.py
@@ -105,18 +105,25 @@
         far = (panel == 1) | ((lax.rem(tile, RUN) >= late) & (lax.rem(la, RUN) != RUN - 1))
         return far & (tile // RUN == la // RUN)
 
+    def straight_from(panel, tile, ca, la):
+        return (panel == 0) & (lax.rem(tile, RUN) == 5) & (ca == 0) & (la > tile)
+
     flows_out, direct_in, shut_out, shut_in = [], [], [], []
     beside = (c < 2) | (c >= nc - 2)
     to_panel_1 = p == 0
     for (la, ca), (dl, dc) in zip(others, AROUND):
         flow, got = on_edge(la, ca), edge
         if dl:
-            flow = flow & ~(on_row(ca) & passed(1 - p, la, l))
-            got = got & ~(on_row(c) & passed(p, l, la))
+            flow = flow & ~(on_row(ca) & passed(1 - p, la, l) & ~straight_from(1 - p, la, ca, l))
+            got = got & ~(on_row(c) & passed(p, l, la) & ~straight_from(p, l, c, la))
         if dc != 1:
             flow = flow & ~((p == 1) & (la == 0) & (lax.rem(ca, 2) == 0))
+        else:
+            flow = flow & ~((p == 1) & (la == 0) & (ca == 0))
         if dc != -1:
             got = got & ~((p == 0) & (l == 0) & (lax.rem(c, 2) == 0))
+        else:
+            got = got & ~((p == 0) & (l == 0) & (c == 0))
         flows_out.append(flow)
         direct_in.append(got)
         shut = ((place == RUN - 1) & (dl <= 0)) | ((place == 0) & (dl == -1))
@@ -128,7 +135,8 @@
             shut = shut | ((l == nl - 1) & ((ca < 2) | (ca >= nc - 2)))
         shut_in.append((p == 0) & shut)
     row_edge = on_row(c)
-    pass_left, pass_right = row_edge & left & passed(p, l - 1, l), row_edge & right & passed(p, l + 1, l)
+    pass_left = row_edge & left & passed(p, l - 1, l) & ~straight_from(p, l - 1, c, l)
+    pass_right = row_edge & right & passed(p, l + 1, l)
     mate_gives = (p == 0) & (l == 0) & (lax.rem(c, 2) == 1)
     mate_takes = (p == 0) & (l == 0) & (lax.rem(c, 2) == 0)
 
@@ -156,6 +164,8 @@
         to_c = jnp.where(by_help, jnp.clip(ca, 2, nc - 3), ca)
         pl.when(direct_in[j] & ~shut_in[j])(lambda: greet(1 - p, to_l, to_c))
 
+    corner, opposite = (p == 0) & (l == 0) & (c == 0), (p == 0) & (l == 0) & (c == nc - 1)
+    pl.when(corner)(lambda: greet(p, l, nc - 1))
     pl.when(near_left)(lambda: greet(p, l - 1, c))
     pl.when(near_right)(lambda: greet(p, l + 1, c))
     pl.when(up)(lambda: greet(p, l, c - 1))
@@ -222,62 +232,6 @@
             at = SHELLS * target + k
             slots[at : at + 1, :] = line if sign > 0 else -line
 
-    def one(flag):
-        return flag.astype(jnp.int32)
-
-    expected = one(up) + one(down) + one(near_left) + one(near_right)
-    for flow, shut in zip(flows_out, shut_out):
-        expected = expected + one(flow & ~shut & ~helped_0)
-    expected = expected + one(helper_1) * (6 + 2 * one(place == RUN - 1)) + 8 * one(helper_0)
-    served = jnp.where(at_helper, 3, 1)
-    at_panel_1 = 2 * served + jnp.where(at_helper, 9, 3)
-    expected = expected + one(end_helper) * jnp.where(p == 1, at_panel_1, 7 * served)
-    pl.semaphore_wait(barrier, expected)
-
-    def remote(src, dst, sent, arrived, *device):
-        return pltpu.make_async_remote_copy(
-            src_ref=src, dst_ref=dst, send_sem=send_sem.at[sent], recv_sem=recv_sem.at[arrived],
-            device_id=device, device_id_type=MESH,
-        )
-
-    slot_copies = [
-        remote(slots, slots_in.at[8 - j], 0, (8 - j) // 3, 1 - p, la, ca) for j, (la, ca) in enumerate(others)
-    ]
-
-    def whole(sent, arrived, sets):
-        return remote(sets, sets, sent, arrived, 1 - p, l, c)
-
-    def send_slots(wave):
-        for j in SEND_ORDER:
-            la, ca = others[j]
-            spot = lax.rem(la, RUN)
-            turn = jnp.where(p == 0, 0, jnp.where(spot == 0, 0, jnp.where(spot < 3, 0, jnp.where(spot < 5, 0, 0))))
-            pl.when(flows_out[j] & ~shut_out[j] & ~helped_0 & (turn == wave))(slot_copies[j].start)
-
-    send_slots(0)
-
-    def tell(*device):
-        pl.semaphore_signal(told, inc=1, device_id=device, device_id_type=MESH)
-
-    @pl.when(helper_0 | helper_1)
-    def _():
-        first = jnp.where(c == 2, 0, nc - 2)
-        for more in range(2):
-            tell(p, jnp.where(p == 0, l + 1, l), first + more)
-
-    @pl.when(end_helper)
-    def _():
-        tell(p, nl - 1, c)
-        pl.when(p == 1)(lambda: tell(p, 0, c))
-
-        @pl.when(at_helper)
-        def _():
-            first = jnp.where(c == 2, 0, nc - 2)
-            for more in range(2):
-                tell(p, nl - 1, first + more)
-                pl.when(p == 1)(lambda: tell(p, 0, first + more))
-                pl.when(p == 1)(lambda: tell(p, nl - 2, first + more))
-
     lanes = lax.broadcasted_iota(jnp.int32, (TALL, CP), 1)
     packed = jnp.zeros((TALL, CP), jnp.float32)
     for f in range(FIELDS):
@@ -290,15 +244,6 @@
     for f in range(FIELDS):
         col_out[1, f] = upright[4 * f : 4 * f + 2]
         col_out[0, f] = upright[4 * f + 2 : 4 * f + 4]
-
-    to_up = remote(row_out.at[0], row_in.at[1], 1, 4, p, l, c - 1)
-    to_down = remote(row_out.at[1], row_in.at[0], 1, 3, p, l, c + 1)
-    to_left = remote(col_out.at[0], col_in.at[1], 2, 6, p, l - 1, c)
-    to_right = remote(col_out.at[1], col_in.at[0], 2, 5, p, l + 1, c)
-    pl.when(near_left)(to_left.start)
-    pl.when(near_right)(to_right.start)
-    pl.when(up)(to_up.start)
-    pl.when(down)(to_down.start)
 
     row0 = (c * CT).astype(jnp.float32) + 0.5
     col0 = (l * CP).astype(jnp.float32) + 0.5
@@ -341,8 +286,6 @@
         acc[7, pl.ds(at, 8), :] = u[7] - (tau * GRAVITY) * (m[0] * er[0] + m[1] * er[1] + m[2] * er[2])
         return 0
 
-    lax.fori_loop(0, TALL // 8, one_block, 0)
-
     ends = {1: 8.0 / 12.0, 2: -1.0 / 12.0}
 
     def gives(along, across, n, step):
@@ -373,7 +316,82 @@
             acc[f, here, :] = acc[f, here, :] - tau * whole
         return 0
 
-    lax.fori_loop(0, FIELDS, one_field, 0)
+    def own_cells():
+        lax.fori_loop(0, TALL // 8, one_block, 0)
+        lax.fori_loop(0, FIELDS, one_field, 0)
+
+    idle = (p == 0) & (place < RUN - 1)
+    pl.when(idle)(own_cells)
+
+    def one(flag):
+        return flag.astype(jnp.int32)
+
+    expected = one(up) + one(down) + one(near_left) + one(near_right)
+    for flow, shut in zip(flows_out, shut_out):
+        expected = expected + one(flow & ~shut & ~helped_0)
+    expected = expected + one(opposite)
+    expected = expected + one(helper_1) * (6 + 2 * one(place == RUN - 1)) + 8 * one(helper_0)
+    served = jnp.where(at_helper, 3, 1)
+    at_panel_1 = 2 * served + jnp.where(at_helper, 9, 3)
+    expected = expected + one(end_helper) * jnp.where(p == 1, at_panel_1, 7 * served)
+    pl.semaphore_wait(barrier, expected)
+
+    def remote(src, dst, sent, arrived, *device):
+        return pltpu.make_async_remote_copy(
+            src_ref=src, dst_ref=dst, send_sem=send_sem.at[sent], recv_sem=recv_sem.at[arrived],
+            device_id=device, device_id_type=MESH,
+        )
+
+    slot_copies = [
+        remote(slots, slots_in.at[8 - j], 0, (8 - j) // 3, 1 - p, la, ca) for j, (la, ca) in enumerate(others)
+    ]
+
+    def whole(sent, arrived, sets):
+        return remote(sets, sets, sent, arrived, 1 - p, l, c)
+
+    def send_slots(wave):
+        for j in SEND_ORDER:
+            la, ca = others[j]
+            spot = lax.rem(la, RUN)
+            turn = jnp.where((p == 0) | ((spot == 5) & (place == 6)), 2, jnp.where(spot == 1, 0, 1))
+            pl.when(flows_out[j] & ~shut_out[j] & ~helped_0 & (turn == wave))(slot_copies[j].start)
+
+    send_slots(0)
+    send_slots(1)
+
+    def tell(*device):
+        pl.semaphore_signal(told, inc=1, device_id=device, device_id_type=MESH)
+
+    @pl.when(helper_0 | helper_1)
+    def _():
+        first = jnp.where(c == 2, 0, nc - 2)
+        for more in range(2):
+            tell(p, jnp.where(p == 0, l + 1, l), first + more)
+
+    @pl.when(end_helper)
+    def _():
+        tell(p, nl - 1, c)
+        pl.when(p == 1)(lambda: tell(p, 0, c))
+
+        @pl.when(at_helper)
+        def _():
+            first = jnp.where(c == 2, 0, nc - 2)
+            for more in range(2):
+                tell(p, nl - 1, first + more)
+                pl.when(p == 1)(lambda: tell(p, 0, first + more))
+                pl.when(p == 1)(lambda: tell(p, nl - 2, first + more))
+
+    to_up = remote(row_out.at[0], row_in.at[1], 1, 4, p, l, c - 1)
+    to_down = remote(row_out.at[1], row_in.at[0], 1, 3, p, l, c + 1)
+    to_left = remote(col_out.at[0], col_in.at[1], 2, 6, p, l - 1, c)
+    to_right = remote(col_out.at[1], col_in.at[0], 2, 5, p, l + 1, c)
+    pl.when(near_left)(to_left.start)
+    pl.when(near_right)(to_right.start)
+    pl.when(up)(to_up.start)
+    pl.when(down)(to_down.start)
+    send_slots(2)
+
+    pl.when(~idle)(own_cells)
 
     @pl.when(helped_0 | helped_1)
     def _():
@@ -442,20 +460,6 @@
             shift = (CP - 2 - 4 * f) % CP
             acc[f] = acc[f] - jnp.where(rim, pltpu.roll(stood, shift, 1) if shift else stood, 0.0)
 
-    pl.when(left)(to_right.wait_recv)
-    pl.when(right)(to_left.wait_recv)
-    pl.when(left & right)(add_columns)
-
-    @pl.when(up)
-    def _():
-        to_down.wait_recv()
-        add_rows(0, [row_in[0, f] for f in range(FIELDS)])
-
-    @pl.when(down)
-    def _():
-        to_up.wait_recv()
-        add_rows(1, [row_in[1, f] for f in range(FIELDS)])
-
     def name(kind, lines):
         for r, line in enumerate(lines):
             named[kind, r] = line
@@ -486,6 +490,24 @@
             for m in range(4):
                 picked[kind, r, 8 * m : 8 * m + 8, :] = found[m]
 
+    def add_panel_rims():
+        pl.when(left)(to_right.wait_recv)
+        pl.when(right)(to_left.wait_recv)
+        pl.when(left & right)(add_columns)
+
+        @pl.when(up)
+        def _():
+            to_down.wait_recv()
+            add_rows(0, [row_in[0, f] for f in range(FIELDS)])
+
+        @pl.when(down)
+        def _():
+            to_up.wait_recv()
+            add_rows(1, [row_in[1, f] for f in range(FIELDS)])
+
+    straight = (p == 0) & (place < 4)
+    pl.when(~straight)(add_panel_rims)
+
     pass_on = [
         remote(slots_in.at[3:6], slots_in.at[6:9], 3, 2, p, l - 1, c),
         remote(slots_in.at[3:6], slots_in.at[0:3], 3, 0, p, l + 1, c),
@@ -494,14 +516,18 @@
         remote(slots_in.at[3 * group : 3 * group + 2], slots_in.at[3 * group + 1 : 3 * group + 3], 4, group, p, l, c - 1)
         for group in range(3)
     ]
+    to_corner = [remote(slots_in.at[3 * g + 1], slots_in.at[3 * g], 4, g, p, l, 0) for g in range(3)]
     for turn, group in enumerate((1, 0, 2)):
         pl.when(edge)(whole(0, group, slots_in.at[3 * group : 3 * group + 3]).wait_recv)
         if group == 1:
             pl.when(pass_left)(pass_on[0].start)
             pl.when(pass_right)(pass_on[1].start)
         pl.when(mate_gives)(to_mate[group].start)
+        pl.when(opposite)(to_corner[group].start)
         pl.when(row_edge)(lambda: pick_ghosts(0, group, turn == 0))
         pl.when(at_end)(lambda: pick_ghosts(1, group, turn == 0))
+
+    pl.when(straight)(add_panel_rims)
 
     @pl.when(at_end)
     def _():
@@ -537,7 +563,8 @@
     wait_sent(1, one(up) + one(down), [row_in.at[0:n] for n in (1, 2)])
     wait_sent(2, one(left) + one(right), [col_in.at[0:n] for n in (1, 2)])
     wait_sent(3, one(pass_left) + one(pass_right), [slots_in.at[0:n] for n in (3, 6)])
-    pl.when(mate_gives)(whole(4, 0, slots_in.at[0:6]).wait_send)
+    pl.when(mate_gives & ~opposite)(whole(4, 0, slots_in.at[0:6]).wait_send)
+    pl.when(opposite)(whole(4, 0, slots_in.at[0:9]).wait_send)
 
 
 def body(state_now, send_row, send_col, send_weight, ghost_slot):

time: 22.9 us -> 22.3 us (0.974)
  the two profiles are of different devices: /device:TPU:32 before, /device:TPU:1 now
where the time goes in v6:
time: 22.3 us; the launch traced here: 22.2 us
  Pallas kernels  21.4 us (96%)
  local copies, waits for them, and re-layouts  0.8 us (4%)
    pallas_call x1, Pallas kernels, body(): pl.pallas_call(kernel, out_shape=pltpu.VMEM((FIELDS, TALL, CP), f32), in_...  21.4 us
    unnamed x1, local copies, waits for them, and re-layouts  0.8 us

profile of v6, /device:TPU:1, one launch (start us, length us, event | category | flops | bytes accessed | tf_op | source)
XLA Modules:
  0.0 22.2 jit_solution(5977705152145330298)
XLA Ops:
  0.0 21.4 %shard_map.55 = f32[8,128,128]{2,1,0:T(8,128)S(1)} custom-call(f32[8,128,128]{2,1,0:T(8,128)} %bitcast.3, s32[1,1,1,128]{3,2,1,0:T(1,128)} %row_hbm.1, s32[1,1,1,128]{3,2,1,0:T(1,128)} %col_hbm.1, f32[1,1,1,4,128]{4,3,2,1,0:T(4,128)} %weight_hbm.1, s32[1,1,1,640]{3,2,1,0:T(1,128)} %ghost_hbm.1), custom_call_target="tpu_custom_call" | custom-call | tf_op jit(solution)/shard_map/pallas_call | solution.py:572
  21.4 0.8 %copy.7 = f32[1,8,4,32,128]{4,3,2,1,0:T(8,128)} copy(f32[1,8,4,32,128]{4,3,2,1,0:T(8,128)S(1)} %bitcast.2) | data formatting | bytes 1048576

commit v7 on v6

--- a/solution.py
+++ b/solution.py
@@ -517,7 +517,7 @@
         for group in range(3)
     ]
     to_corner = [remote(slots_in.at[3 * g + 1], slots_in.at[3 * g], 4, g, p, l, 0) for g in range(3)]
-    for turn, group in enumerate((1, 0, 2)):
+    for turn, group in enumerate((1, 2, 0)):
         pl.when(edge)(whole(0, group, slots_in.at[3 * group : 3 * group + 3]).wait_recv)
         if group == 1:
             pl.when(pass_left)(pass_on[0].start)

time: 22.3 us -> 22.3 us (level)
  no operation moved by 1% of the time
where the time goes in v7:
time: 22.3 us; the launch traced here: 22.2 us
  Pallas kernels  21.4 us (96%)
  local copies, waits for them, and re-layouts  0.8 us (4%)
    pallas_call x1, Pallas kernels, body(): pl.pallas_call(kernel, out_shape=pltpu.VMEM((FIELDS, TALL, CP), f32), in_...  21.4 us
    unnamed x1, local copies, waits for them, and re-layouts  0.8 us

profile of v7, /device:TPU:1, one launch (start us, length us, event | category | flops | bytes accessed | tf_op | source)
XLA Modules:
  0.0 22.2 jit_solution(2652939156368175525)
XLA Ops:
  0.0 21.4 %shard_map.55 = f32[8,128,128]{2,1,0:T(8,128)S(1)} custom-call(f32[8,128,128]{2,1,0:T(8,128)} %bitcast.3, s32[1,1,1,128]{3,2,1,0:T(1,128)} %row_hbm.1, s32[1,1,1,128]{3,2,1,0:T(1,128)} %col_hbm.1, f32[1,1,1,4,128]{4,3,2,1,0:T(4,128)} %weight_hbm.1, s32[1,1,1,640]{3,2,1,0:T(1,128)} %ghost_hbm.1), custom_call_target="tpu_custom_call" | custom-call | tf_op jit(solution)/shard_map/pallas_call | solution.py:572
  21.4 0.8 %copy.7 = f32[1,8,4,32,128]{4,3,2,1,0:T(8,128)} copy(f32[1,8,4,32,128]{4,3,2,1,0:T(8,128)S(1)} %bitcast.2) | data formatting | bytes 1048576

commit v8 on v6

--- a/solution.py
+++ b/solution.py
@@ -81,14 +81,14 @@
         return (la == 0) | (la == nl - 1) | on_row(ca)
 
     small = [
-        pltpu.make_async_copy(src, dst, in_sem.at[2 + i])
+        pltpu.make_async_copy(src, dst, in_sem.at[3 + i])
         for i, (src, dst) in enumerate(
             ((row_hbm, rows), (col_hbm, cols), (weight_hbm, weight), (ghost_hbm, wanted))
         )
     ]
-    half = FIELDS // 2
+    cuts = (0, 4, 6, 8)
     large = [
-        pltpu.make_async_copy(x_hbm.at[half * i : half * (i + 1)], x.at[half * i : half * (i + 1)], in_sem.at[i]) for i in range(2)
+        pltpu.make_async_copy(x_hbm.at[i:k], x.at[i:k], in_sem.at[n]) for n, (i, k) in enumerate(zip(cuts, cuts[1:]))
     ]
     for load in small + large:
         load.start()
@@ -217,8 +217,8 @@
         return jnp.where(low, a + pltpu.roll(a, 6, 0), b + pltpu.roll(b, 2, 0))
 
     for f in range(FIELDS):
-        if f % half == 0:
-            large[f // half].wait()
+        if f in cuts:
+            large[cuts.index(f)].wait()
         target, sign = TURNED[f]
         sums = []
         for k in range(SHELLS):
@@ -591,7 +591,7 @@
             pltpu.VMEM((FIELDS, TALL, CP), f32),
             pltpu.VMEM((2, 2, FIELDS * SHELLS, CP), f32),
             pltpu.VMEM((2, 2, 8, CP), i32),
-            pltpu.SemaphoreType.DMA((6,)),
+            pltpu.SemaphoreType.DMA((7,)),
             pltpu.SemaphoreType.DMA((5,)),
             pltpu.SemaphoreType.DMA((7,)),
             pltpu.SemaphoreType.REGULAR,

time: 22.3 us -> 22.4 us (level)
  no operation moved by 1% of the time
where the time goes in v8:
time: 22.4 us; the launch traced here: 22.3 us
  Pallas kernels  21.5 us (96%)
  local copies, waits for them, and re-layouts  0.8 us (4%)
    pallas_call x1, Pallas kernels, body(): pl.pallas_call(kernel, out_shape=pltpu.VMEM((FIELDS, TALL, CP), f32), in_...  21.5 us
    unnamed x1, local copies, waits for them, and re-layouts  0.8 us

profile of v8, /device:TPU:1, one launch (start us, length us, event | category | flops | bytes accessed | tf_op | source)
XLA Modules:
  0.0 22.3 jit_solution(12962242339277404916)
XLA Ops:
  0.0 21.5 %shard_map.55 = f32[8,128,128]{2,1,0:T(8,128)S(1)} custom-call(f32[8,128,128]{2,1,0:T(8,128)} %bitcast.3, s32[1,1,1,128]{3,2,1,0:T(1,128)} %row_hbm.1, s32[1,1,1,128]{3,2,1,0:T(1,128)} %col_hbm.1, f32[1,1,1,4,128]{4,3,2,1,0:T(4,128)} %weight_hbm.1, s32[1,1,1,640]{3,2,1,0:T(1,128)} %ghost_hbm.1), custom_call_target="tpu_custom_call" | custom-call | tf_op jit(solution)/shard_map/pallas_call | solution.py:572
  21.5 0.8 %copy.7 = f32[1,8,4,32,128]{4,3,2,1,0:T(8,128)} copy(f32[1,8,4,32,128]{4,3,2,1,0:T(8,128)S(1)} %bitcast.2) | data formatting | bytes 1048576
